TPU v7x, 128 devices: a whole 4x4x4 slice. The times are simulated.
128 devices in a mesh: grp: 4 (over y_hi, core), dev: 32 (over x, z, y_lo).
Axes of the slice: x: 4, y: 4 (y_hi: 2, y_lo: 2; y = y_hi * 2 + y_lo), z: 4, core: 2. Of those that a mesh axis runs over, the one named last changes fastest.
Arguments:
- x_feat: float32 [64, 32768], P(None, 'dev'), may hold values from -4 to 4
- y_feat: float32 [64, 65536], P(None, ('grp', 'dev')), may hold values from -4 to 4
Outputs:
- dual_row: float32 [32768], P('dev')
- dual_col: float32 [65536], P('grp')
All inputs are finite; a program needn't handle non-finite values.
Results may differ from a plain program's by a relative error of at most 0.0003.
Values sent between devices are 32-bit elements; how exact they have to be, the bound alone decides.
No kernel may reach another device: no remote copies, remote signals or barrier semaphores. Data moves between devices by JAX's collectives and lax.ppermute only.
A program may use at most 64 MiB of HBM per device.

v0:
```python
import math

import jax
import jax.numpy as jnp
from jax import lax
from jax.sharding import PartitionSpec as P

ITERS = 2


eps_value = 0.5
block_width = 1024


def combined_all(value, axis, join):
    pieces = jax.tree.map(lambda part: lax.all_gather(part, axis), value)
    head = jax.tree.map(lambda part: part[0], pieces)
    tail = jax.tree.map(lambda part: part[1:], pieces)
    subtotal, _ = lax.scan(lambda subtotal, share: (join(subtotal, share), None), head, tail)
    return subtotal


def pair_cost(source, source_sq, target):
    target_sq = jnp.sum(target * target, axis=0)
    cross = lax.dot_general(
        source,
        target,
        (((0,), (0,)), ((), ())),
        precision=lax.Precision.HIGHEST,
        preferred_element_type=jnp.float32,
    )
    return source_sq[:, None] + target_sq[None, :] - 2.0 * cross


def split_blocks(target, dual):
    width = target.shape[1]
    step = min(block_width, width)
    count = width // step
    return (
        target.reshape(target.shape[0], count, step).transpose(1, 0, 2),
        dual.reshape(count, step),
    )


def combine_lse(first, second):
    peak = jnp.maximum(first[0], second[0])
    total = first[1] * jnp.exp(first[0] - peak) + second[1] * jnp.exp(second[0] - peak)
    return (peak, total)


def row_partial(source, source_sq, blocks, dual):
    duals = dual.reshape(blocks.shape[0], blocks.shape[2])
    rows = source.shape[1]

    def advance(carry, item):
        peak, total = carry
        tblock, dblock = item
        score = (dblock[None, :] - pair_cost(source, source_sq, tblock)) / eps_value
        new_peak = jnp.maximum(peak, jnp.max(score, axis=1))
        total = total * jnp.exp(peak - new_peak) + jnp.sum(
            jnp.exp(score - new_peak[:, None]), axis=1
        )
        return ((new_peak, total), None)

    init = (jnp.full((rows,), -1e30, jnp.float32), jnp.zeros((rows,), jnp.float32))
    result, unused = lax.scan(advance, init, (blocks, duals))
    return result


def col_partial(source, source_sq, blocks, dual):

    def column_block(tblock):
        score = (dual[:, None] - pair_cost(source, source_sq, tblock)) / eps_value
        peak = jnp.max(score, axis=0)
        total = jnp.sum(jnp.exp(score - peak[None, :]), axis=0)
        return (peak, total)

    peak, total = lax.map(column_block, blocks)
    return (peak.reshape(-1), total.reshape(-1))


def on_device(x_feat, y_feat):
    targets = lax.all_gather(y_feat, "dev", axis=1, tiled=True)
    dev_count = lax.axis_size("dev")
    grp_count = lax.axis_size("grp")
    rows = x_feat.shape[1]
    cols = targets.shape[1]
    log_src = math.log(rows * dev_count)
    log_tgt = math.log(cols * grp_count)
    source_sq = jnp.sum(x_feat * x_feat, axis=0)
    blocks, unused = split_blocks(targets, jnp.zeros((cols,), jnp.float32))
    dual_col = jnp.zeros((cols,), jnp.float32)
    dual_row = jnp.zeros((rows,), jnp.float32)
    for iteration in range(ITERS):
        peak, total = row_partial(x_feat, source_sq, blocks, dual_col)
        peak, total = combined_all((peak, total), "grp", combine_lse)
        dual_row = -eps_value * (peak + jnp.log(total)) + eps_value * log_tgt
        peak, total = col_partial(x_feat, source_sq, blocks, dual_row)
        top_all = lax.pmax(peak, "dev")
        summed = lax.psum(total * jnp.exp(peak - top_all), "dev")
        dual_col = -eps_value * (top_all + jnp.log(summed)) + eps_value * log_src
    return (dual_row, dual_col)


def solution(mesh):
    in_specs = (P(None, "dev"), P(None, ("grp", "dev")))
    out_specs = (P("dev"), P("grp"))
    return jax.shard_map(
        on_device, mesh=mesh, in_specs=in_specs, out_specs=out_specs, check_vma=False
    )
```

profile of v0, /device:TPU:1, one launch (start us, length us, event | category | flops | bytes accessed | tf_op | source)
XLA Modules:
  0.0 1905.6 jit_solution(8454041696228979872)
XLA Ops:
  8.9 141.4 %all-gather.6.cloned.1.call-done = f32[64,16384]{1,0:T(8,128)} async-done(((f32[64,512]{1,0:T(8,128)}), f32[64,16384]{1,0:T(8,128)}) %all-gather.6.cloned.1.call-update) | async-done | bytes 4194320 | tf_op jit(solution)/shard_map/all_gather | solution.py:83
  159.3 179.2 %while.78 = (s32[]{:T(128)}, f32[1024]{0:T(1024)S(1)}, f32[1024]{0:T(1024)S(1)}, f32[1024]{0:T(1024)S(1)}, f32[16,64,1024]{2,1,0:T(8,128)}, /*index=5*/f32[64,1024]{1,0:T(8,128)S(1)}, s32[]{:T(128)}, s32[]{:T(128)}) while((s32[]{:T(128)}, f32[1024]{0:T(1024)S(1)}, f32[1024]{0:T(1024)S(1)}, f32[1024]{0:T(1024)S(1)}, ...), condition=%wide.region_5.6_spmd.clone, body=%wide.region_1.5_spmd.clone.sunk | while | flops 819073024 | bytes 9249380 | solution.py:66
  171.5 6.7 fusion.60
  205.1 6.7 fusion.60
  294.7 6.7 fusion.60
  338.5 27.3 %all-gather = f32[4096]{0:T(1024)S(1)} all-gather(f32[1024]{0:T(1024)S(1)} %get-tuple-element.205), channel_id=2, replica_groups=mesh['grp'=4,'dev'=32] {'grp'}, dimensions={0}, use_global_device_ids=true | all-gather | bytes 20480 | tf_op jit(solution)/shard_map/all_gather | solution.py:16
  365.8 6.9 all-gather.1
  372.9 131.3 %while.75 = (s32[]{:T(128)}, f32[16,1024]{1,0:T(8,128)S(1)}, f32[16,1024]{1,0:T(8,128)S(1)}, f32[1024]{0:T(1024)S(1)}, f32[1024]{0:T(1024)S(1)}, /*index=5*/f32[...) while((s32[]{:T(128)}, f32[16,1024]{1,0:T(8,128)S(1)}, f32[16,1024]{1,0:T(8,128)S(1)}, ...), condition=%wide.region_12.13_spmd, body=%wide.region_8.12_spmd.sunk | while | flops 819065856 | bytes 9233001 | solution.py:78
  505.0 257.2 %all-reduce.5.cloned.1.call-done = f32[16384]{0:T(1024)} async-done(((f32[16384]{0:T(1024)}), f32[16384]{0:T(1024)}) %all-reduce.5.cloned.1.call-update) | async-done | bytes 65552 | tf_op jit(solution)/shard_map/pmax | solution.py:99
  763.8 270.9 %all-reduce.7.cloned.1.call-done = f32[16384]{0:T(1024)} async-done(((f32[16384]{0:T(1024)}), f32[16384]{0:T(1024)}) %all-reduce.7.cloned.1.call-update) | async-done | bytes 65552 | tf_op jit(solution)/shard_map/psum | solution.py:100
  1035.7 174.3 %while.79 = (s32[]{:T(128)}, f32[1024]{0:T(1024)S(1)}, f32[1024]{0:T(1024)S(1)}, f32[16,1024]{1,0:T(8,128)S(1)}, f32[1024]{0:T(1024)S(1)}, /*index=5*/f32[16,64,...) while((s32[]{:T(128)}, f32[1024]{0:T(1024)S(1)}, f32[1024]{0:T(1024)S(1)}, ...), condition=%wide.region_19.20_spmd.clone, body=%wide.region_15.19_spmd.clone.sunk | while | flops 819073024 | bytes 9265776 | solution.py:66
  1036.7 6.7 fusion.64
  1047.6 6.7 fusion.64
  1058.5 6.7 fusion.64
  1069.4 6.7 fusion.64
  1080.3 6.7 fusion.64
  1091.2 6.7 fusion.64
  1102.1 6.7 fusion.64
  1112.9 6.7 fusion.64
  1123.8 6.7 fusion.64
  1134.7 6.7 fusion.64
  1145.6 6.7 fusion.64
  1156.5 6.7 fusion.64
  1167.4 6.7 fusion.64
  1178.3 6.7 fusion.64
  1189.2 6.7 fusion.64
  1200.1 6.7 fusion.64
  1210.0 22.2 %all-gather.2 = f32[4096]{0:T(1024)S(1)} all-gather(f32[1024]{0:T(1024)S(1)} %get-tuple-element.211), channel_id=4, replica_groups=mesh['grp'=4,'dev'=32] {'grp'}, dimensions={0}, use_global_device_ids=true | all-gather | bytes 20480 | tf_op jit(solution)/shard_map/all_gather | solution.py:16
  1232.2 6.9 all-gather.3
  1239.3 131.3 %while.77 = (s32[]{:T(128)}, f32[16,1024]{1,0:T(8,128)S(1)}, f32[16,1024]{1,0:T(8,128)S(1)}, f32[1024]{0:T(1024)S(1)}, f32[1024]{0:T(1024)S(1)}, /*index=5*/f32[...) while((s32[]{:T(128)}, f32[16,1024]{1,0:T(8,128)S(1)}, f32[16,1024]{1,0:T(8,128)S(1)}, ...), condition=%wide.region_26.27_spmd, body=%wide.region_22.26_spmd.sunk | while | flops 819065856 | bytes 9233001 | solution.py:78
  1371.4 253.7 %all-reduce.9.cloned.1.call-done = f32[16384]{0:T(1024)} async-done(((f32[16384]{0:T(1024)}), f32[16384]{0:T(1024)}) %all-reduce.9.cloned.1.call-update) | async-done | bytes 65552 | tf_op jit(solution)/shard_map/pmax | solution.py:99
  1626.7 270.8 %all-reduce.11.cloned.1.call-done = f32[16384]{0:T(1024)} async-done(((f32[16384]{0:T(1024)}), f32[16384]{0:T(1024)}) %all-reduce.11.cloned.1.call-update) | async-done | bytes 65552 | tf_op jit(solution)/shard_map/psum | solution.py:100
  (411 shorter events, 504.1 us)
Async XLA Ops:
  7.2 143.2 %all-gather.6.cloned.1.call-start = ((), (), s32[]{:S(2)}) async-start(), calls=%async_computation | async-start | bytes 4325376 | tf_op jit(solution)/shard_map/all_gather | solution.py:83
  7.9 754.3 %all-reduce.5.cloned.1.call-start = ((), (), s32[]{:S(2)}) async-start(), calls=%async_computation.1 | async-start | bytes 131072 | tf_op jit(solution)/shard_map/pmax | solution.py:99
  154.9 4.4 copy-start
  504.9 529.9 %all-reduce.7.cloned.1.call-start = ((), (), s32[]{:S(2)}) async-start(), calls=%async_computation.2 | async-start | bytes 131072 | tf_op jit(solution)/shard_map/psum | solution.py:100
  763.8 861.4 %all-reduce.9.cloned.1.call-start = ((), (), s32[]{:S(2)}) async-start(), calls=%async_computation.3 | async-start | bytes 131072 | tf_op jit(solution)/shard_map/pmax | solution.py:99
  1370.7 528.4 %copy-start.1 = (f32[1024]{0:T(1024)}, f32[1024]{0:T(1024)S(1)}, u32[]{:S(2)}) copy-start(f32[1024]{0:T(1024)S(1)} %get-tuple-element.832) | copy-start | bytes 12292
  1371.4 526.2 %all-reduce.11.cloned.1.call-start = ((), (), s32[]{:S(2)}) async-start(), calls=%async_computation.4 | async-start | bytes 131072 | tf_op jit(solution)/shard_map/psum | solution.py:100
Sparse Core Ops, SparseCore 0:
  9.6 140.6 all-gather.5
  505.0 257.1 all-reduce.4
  765.4 269.2 all-reduce.6
  1371.5 253.6 all-reduce.8
  1628.2 269.2 all-reduce.10
where the time goes:
time: 1920 us; the launch traced here: 1910 us
  waiting for transfers between devices  1190 us (62%)
  matrix products  380 us (20%)
  other arithmetic  233 us (12%)
  blocking collectives  63.3 us (3%)
    psum x2, waiting for transfers between devices, on_device(): summed = lax.psum(total * jnp.exp(peak - top_all), 'dev')  542 us
    pmax x2, waiting for transfers between devices, on_device(): top_all = lax.pmax(peak, 'dev')  511 us
    dot_general x64, matrix products, pair_cost(): lax.dot_general(source, target, (((0,), (0,)), ((), ())), precision=lax.P...  380 us
    all_gather x1, waiting for transfers between devices, on_device(): targets = lax.all_gather(y_feat, 'dev', axis=1, tiled=True)  141 us
    reduce_sum x32, other arithmetic, advance(): jnp.sum(jnp.exp(score - new_peak[:, None]), axis=1)  106 us
    all_gather x4, blocking collectives, combined_all(): pieces = jax.tree.map(lambda part: lax.all_gather(part, axis), value)  63.3 us
    reduce_sum x64, other arithmetic, pair_cost(): target_sq = jnp.sum(target * target, axis=0)  63 us
    reduce_sum x32, other arithmetic, column_block(): total = jnp.sum(jnp.exp(score - peak[None, :]), axis=0)  57.2 us
  transfers between devices with their start and end apart: 5, of which 5 were waited for; matrix products, arithmetic and copies ran while one was open for 0% of the time, Pallas kernels for 0%

commit v1 on v0

v1 whole, which is shorter than its diff:
```python
import math

import jax
import jax.numpy as jnp
from jax import lax
from jax.experimental import pallas as pl
from jax.experimental.pallas import tpu as pltpu
from jax.sharding import Mesh
from jax.sharding import PartitionSpec as P

ITERS = 2
EPS = 0.5
LOG2E = 1.0 / math.log(2.0)
SCALE = LOG2E / EPS

LANES = 128
CHUNK = 256
WIDTH = 256
ACC_ROWS = 16
DUAL_LANE = 64

f32 = jnp.float32
bf16 = jnp.bfloat16
vmem = pl.BlockSpec(memory_space=pltpu.VMEM)


def split2(value):
    high = value.astype(bf16)
    return high, (value - high.astype(f32)).astype(bf16)


def fold(op, acc, value):
    rows = acc.shape[0]
    for i in range(value.shape[0] // rows):
        acc = op(acc, value[i * rows : (i + 1) * rows])
    return acc


def prepare_side(src, main, tail, rhs, norm, scale):
    blocks, dim, cells = src.shape
    for b in range(blocks):
        value = src[b]
        square = jnp.sum(value * value, axis=0, keepdims=True)
        for q in range(cells // LANES):
            row = b * (cells // LANES) + q
            norm[row : row + 1, :] = square[:, q * LANES : (q + 1) * LANES]
        high, low = split2(value * scale)
        here = pl.ds(b * cells, cells)
        rhs[0:dim, here] = high
        rhs[dim : 2 * dim, here] = low
        rhs[2 * dim : 3 * dim, here] = high
        place = lax.broadcasted_iota(jnp.int32, (dim, cells), 0)
        rhs[3 * dim : 4 * dim, here] = jnp.where(place < 3, 1.0, 0.0).astype(bf16)
        main[here, :] = jnp.transpose(jnp.concatenate([high, high], axis=0))
        tail[here, :] = jnp.transpose(jnp.concatenate([low, jnp.zeros_like(low)], axis=0))


def prepare_kernel(log_src, x_ref, y_ref, xm, xt, xr, xn, ym, yt, yr, yn, first):
    prepare_side(x_ref, xm, xt, xr, xn, 2.0 * SCALE)
    prepare_side(y_ref, ym, yt, yr, yn, 1.0)
    first[0] = log_src + SCALE * yn[...]


def combine(parts, log_count):
    peak = parts[0]
    for i in range(1, parts.shape[0]):
        peak = jnp.maximum(peak, parts[i])
    total = jnp.exp2(parts[0] - peak)
    for i in range(1, parts.shape[0]):
        total = total + jnp.exp2(parts[i] - peak)
    return log_count - (peak + jnp.log2(total))


def pass_kernel(log_count, parts, main, tail, rhs, out, *rest):
    full, score = rest[-2:]
    length, width = main.shape[0], rhs.shape[1]
    dual = combine(parts, log_count)
    if len(rest) == 4:
        norm, dual_out = rest[:2]
        dual_out[...] = dual * (1.0 / SCALE) + norm[...]
    high = dual.astype(bf16).astype(f32)
    mid = (dual - high).astype(bf16).astype(f32)
    low = dual - high - mid
    place = lax.broadcasted_iota(jnp.int32, (LANES, LANES), 0)
    for k in range(length // LANES):
        here = pl.ds(k * LANES, LANES)
        rows = jnp.where(place == DUAL_LANE, high[k : k + 1], 0.0)
        rows = jnp.where(place == DUAL_LANE + 1, mid[k : k + 1], rows)
        rows = jnp.where(place == DUAL_LANE + 2, low[k : k + 1], rows)
        full[here, :] = (tail[here, :].astype(f32) + jnp.transpose(rows)).astype(bf16)

    def scores(block, chunk, peak):
        here = pl.ds(chunk * CHUNK, CHUNK)
        lhs = jnp.concatenate([main[here, :], full[here, :]], axis=1)
        cols = pl.ds(pl.multiple_of(block * WIDTH, WIDTH), WIDTH)
        value = jnp.dot(lhs, rhs[:, cols], preferred_element_type=f32)
        score[here, :] = value
        return fold(jnp.maximum, peak, value)

    def sums(chunk, top, acc):
        here = pl.ds(chunk * CHUNK, CHUNK)
        return fold(jnp.add, acc, jnp.exp2(score[here, :] - top))

    def finish(block, top, acc):
        value = top + jnp.log2(jnp.sum(acc, axis=0, keepdims=True))
        for q in range(WIDTH // LANES):
            row = block * (WIDTH // LANES) + q
            piece = value[:, q * LANES : (q + 1) * LANES][None]
            out[:, pl.ds(row, 1), :] = jnp.broadcast_to(piece, (out.shape[0], 1, LANES))

    chunks, blocks = length // CHUNK, width // WIDTH
    lowest = jnp.full((ACC_ROWS, WIDTH), -jnp.inf, f32)
    zero = jnp.zeros((ACC_ROWS, WIDTH), f32)

    peak = lowest
    for chunk in range(chunks):
        peak = scores(0, chunk, peak)

    def step(block, top):
        peak, acc = lowest, zero
        for chunk in range(chunks):
            acc = sums(chunk, top, acc)
            peak = scores(block, chunk, peak)
        finish(block - 1, top, acc)
        return jnp.max(peak, axis=0, keepdims=True)

    top = lax.fori_loop(1, blocks, step, jnp.max(peak, axis=0, keepdims=True))
    acc = zero
    for chunk in range(chunks):
        acc = sums(chunk, top, acc)
    finish(blocks - 1, top, acc)


def final_kernel(log_count, parts, norm, out):
    value = combine(parts, log_count) * (1.0 / SCALE) + norm[...]
    for i in range(out.shape[0]):
        out[i] = value


def params(mib):
    return pltpu.CompilerParams(vmem_limit_bytes=mib * 2**20)


def lse_pass(log_count, parts, main, tail, rhs, copies, norm=None):
    length, width = main.shape[0], rhs.shape[1]
    out = jax.ShapeDtypeStruct((copies, width // LANES, LANES), f32)
    scratch = [pltpu.VMEM((length, LANES), bf16), pltpu.VMEM((length, WIDTH), f32)]
    if norm is None:
        return pl.pallas_call(
            lambda *refs: pass_kernel(log_count, *refs),
            out_shape=out,
            in_specs=[vmem] * 4,
            out_specs=vmem,
            scratch_shapes=scratch,
            compiler_params=params(20),
        )(parts, main, tail, rhs)

    def kernel(parts, main, tail, rhs, norm, out, dual_out, full, score):
        pass_kernel(log_count, parts, main, tail, rhs, out, norm, dual_out, full, score)

    return pl.pallas_call(
        kernel,
        out_shape=(out, jax.ShapeDtypeStruct((length // LANES, LANES), f32)),
        in_specs=[vmem] * 5,
        out_specs=(vmem, vmem),
        scratch_shapes=scratch,
        compiler_params=params(20),
    )(parts, main, tail, rhs, norm)


def gathered(value, axes):
    copies = jnp.broadcast_to(value[None], (lax.axis_size(axes),) + value.shape)
    return lax.all_to_all(copies, axes, 0, 0, tiled=True)


def exchanged(parts, axes):
    return lax.all_to_all(parts, axes, 0, 0, tiled=True)


ROW_GATHER = "x"
COL_GATHER = ("z", "yl")
ROW_PEERS = ("yh", "core", "x")
COL_PEERS = ("z", "yl")


def on_device(x_feat, y_feat):
    xg = gathered(x_feat, ROW_GATHER)
    yg = gathered(y_feat, COL_GATHER)
    rows, cols = xg.shape[0] * xg.shape[2], yg.shape[0] * yg.shape[2]
    row_peers, col_peers = lax.axis_size(ROW_PEERS), lax.axis_size(COL_PEERS)
    log_tgt = math.log2(cols * row_peers)
    log_src = math.log2(rows * col_peers)

    def side(cells):
        return [
            jax.ShapeDtypeStruct((cells, LANES), bf16),
            jax.ShapeDtypeStruct((cells, LANES), bf16),
            jax.ShapeDtypeStruct((4 * x_feat.shape[0], cells), bf16),
            jax.ShapeDtypeStruct((cells // LANES, LANES), f32),
        ]

    xm, xt, xr, xn, ym, yt, yr, yn, parts = pl.pallas_call(
        lambda *refs: prepare_kernel(log_src, *refs),
        out_shape=side(rows) + side(cols) + [jax.ShapeDtypeStruct((1, cols // LANES, LANES), f32)],
        in_specs=[vmem] * 2,
        out_specs=[vmem] * 9,
        compiler_params=params(20),
    )(xg, yg)
    for iteration in range(ITERS):
        parts = exchanged(lse_pass(log_src, parts, ym, yt, xr, row_peers), ROW_PEERS)
        sums, dual_row = lse_pass(log_tgt, parts, xm, xt, yr, col_peers, xn)
        parts = exchanged(sums, COL_PEERS)
    own = x_feat.shape[1] // LANES
    dual_row = lax.dynamic_slice_in_dim(dual_row, lax.axis_index(ROW_GATHER) * own, own, 0)
    spread = lax.axis_size(ROW_GATHER)
    dual_col = pl.pallas_call(
        lambda *refs: final_kernel(log_src, *refs),
        out_shape=jax.ShapeDtypeStruct((spread, cols // LANES, LANES), f32),
        in_specs=[vmem] * 2,
        out_specs=vmem,
    )(parts, yn)
    dual_col = exchanged(dual_col, ROW_GATHER)
    return dual_row.reshape(-1), dual_col.reshape(-1)


def solution(mesh):
    fine = Mesh(mesh.devices.reshape(2, 2, 4, 4, 2), ("yh", "core", "x", "z", "yl"))
    dev = ("x", "z", "yl")
    in_specs = (P(None, dev), P(None, ("yh", "core") + dev))
    out_specs = (P(dev), P(("yh", "core")))
    return jax.shard_map(
        on_device, mesh=fine, in_specs=in_specs, out_specs=out_specs, check_vma=False
    )
```

time: 1920 us -> 157 us (0.08)
  waiting for transfers between devices: 1190 us -> 9.3 us
  matrix products: 380 us -> 0 us
  other arithmetic: 233 us -> 0 us
  Pallas kernels: 0 us -> 59.2 us
    psum x2 -> x0, waiting for transfers between devices: 542 us -> none  [on_device(): summed = lax.psum(total * jnp.exp(peak - top_all), 'dev')]
    pmax x2 -> x0, waiting for transfers between devices: 511 us -> none  [on_device(): top_all = lax.pmax(peak, 'dev')]
    dot_general x64 -> x0, matrix products: 380 us -> none  [pair_cost(): lax.dot_general(source, target, (((0,), (0,)), ((), ())), precision=lax.P...]
    reduce_sum x129 -> x0, other arithmetic: 227 us -> none  [the longest x32 106 us: advance(): jnp.sum(jnp.exp(score - new_peak[:, None]), axis=1)]
    all_gather x1 -> x0, waiting for transfers between devices: 141 us -> none  [on_device(): targets = lax.all_gather(y_feat, 'dev', axis=1, tiled=True)]
    all_to_all x0 -> x5, blocking collectives: none -> 76 us  [the longest x2 38.1 us: gathered(): return lax.all_to_all(copies, axes, 0, 0, tiled=True)]
    all_gather x4 -> x0, blocking collectives: 63.3 us -> none  [combined_all(): pieces = jax.tree.map(lambda part: lax.all_gather(part, axis), value)]
    pallas_call x0 -> x6, Pallas kernels: none -> 59.2 us  [the longest x2 28.4 us: lse_pass(): pl.pallas_call(kernel, out_shape=(out, jax.ShapeDtypeStruct((length // LA...]
  transfers between devices with their start and end apart: 5 -> 2, of which waited for: 5 -> 2; matrix products, arithmetic and copies ran while one was open for 0% -> 0% of each run, Pallas kernels for 0% -> 0%
where the time goes in v1:
time: 157 us; the launch traced here: 155 us
  blocking collectives  76 us (48%)
  Pallas kernels  59.2 us (38%)
  waiting for transfers between devices  9.3 us (6%)
  starting transfers between devices  6.65 us (4%)
  local copies, waits for them, and re-layouts  3.1 us (2%)
    all_to_all x2, blocking collectives, gathered(): return lax.all_to_all(copies, axes, 0, 0, tiled=True)  38.1 us
    all_to_all x3, blocking collectives, exchanged(): return lax.all_to_all(parts, axes, 0, 0, tiled=True)  38 us
    pallas_call x2, Pallas kernels, lse_pass(): pl.pallas_call(kernel, out_shape=(out, jax.ShapeDtypeStruct((length // LA...  28.4 us
    pallas_call x2, Pallas kernels, lse_pass(): pl.pallas_call(lambda *refs: pass_kernel(log_count, *refs), out_shape=out...  28 us
    all_to_all x2, waiting for transfers between devices, exchanged(): return lax.all_to_all(parts, axes, 0, 0, tiled=True)  9.3 us
    all_to_all x2, starting transfers between devices, exchanged(): return lax.all_to_all(parts, axes, 0, 0, tiled=True)  6.65 us
  transfers between devices with their start and end apart: 2, of which 2 were waited for; matrix products, arithmetic and copies ran while one was open for 0% of the time, Pallas kernels for 0%

profile of v1, /device:TPU:1, one launch (start us, length us, event | category | flops | bytes accessed | tf_op | source)
XLA Modules:
  0.0 155.1 jit_solution(9672515669831293567)
XLA Ops:
  0.6 0.0 copy-start.2
  0.6 1.1 broadcast_in_dim.4
  1.7 18.8 %all_to_all.35.refs_0_ = f32[4,64,1024]{2,1,0:T(8,128)S(1)} all-to-all(f32[4,64,1024]{2,1,0:T(8,128)S(1)} %broadcast_in_dim.4), channel_id=1, replica_groups=mesh['yh'=2,'core'=2,'x'=4,'z'=4,'yl'=2] {'x'}, dimensions={0} | all-to-all | bytes 2097152 | tf_op jit(solution)/shard_map/all_to_all | solution.py:173
  20.6 0.0 copy-done.2
  20.6 0.1 broadcast_in_dim.5
  20.7 19.2 %all_to_all.36.refs_1_ = f32[8,64,512]{2,1,0:T(8,128)S(1)} all-to-all(f32[8,64,512]{2,1,0:T(8,128)S(1)} %broadcast_in_dim.5), channel_id=1, replica_groups=mesh['yh'=2,'core'=2,'x'=4,'z'=4,'yl'=2] {'z','yl'}, dimensions={0} | all-to-all | bytes 2097152 | tf_op jit(solution)/shard_map/all_to_all | solution.py:173
  39.9 1.3 shard_map.41
  41.2 0.0 copy-start
  41.2 14.0 %shard_map.42 = f32[16,32,128]{2,1,0:T(8,128)S(1)} custom-call(f32[1,32,128]{2,1,0:T(8,128)S(1)} %get-tuple-element.14.refs_0_, bf16[4096,128]{1,0:T(8,128)(2,1)S(1)} %get-tuple-element.15.refs_1_, bf16[4096,128]{1,0:T(8,128)(2,1)S(1)} %get-tuple-element.16.refs_2_, bf16[256,4096]{1,0:T(8,128)(2,1)S(1)} %get-tuple-element.17.refs_3_), custom_call_target="tpu_custom_call" | custom-call | tf_op jit(solution)/shard_map/pallas_call | solution.py:149
  55.2 0.0 copy-done
  55.2 16.7 %all_to_all.37.parts = f32[16,32,128]{2,1,0:T(8,128)S(1)} all-to-all(f32[16,32,128]{2,1,0:T(8,128)S(1)} %shard_map.42), channel_id=1, replica_groups=mesh['yh'=2,'core'=2,'x'=4,'z'=4,'yl'=2] {'yh','core','x'}, dimensions={0} | all-to-all | bytes 524288 | tf_op jit(solution)/shard_map/all_to_all | solution.py:177
  71.9 13.9 %shard_map.43 = (f32[8,32,128]{2,1,0:T(8,128)S(1)}, f32[32,128]{1,0:T(8,128)}) custom-call(f32[16,32,128]{2,1,0:T(8,128)S(1)} %all_to_all.37.parts, bf16[4096,128]{1,0:T(8,128)(2,1)S(1)} %get-tuple-element.18.main, bf16[4096,128]{1,0:T(8,128)(2,1)S(1)} %get-tuple-element.19.tail, bf16[256,4096]{1,0:T(8,128)(2,1)S(1)} %get-tuple-element.20.rhs, ...), custom_call_target="tpu_custom_call" | custom-call | tf_op jit(solution)/shard_map/pallas_call | solution.py:161
  85.8 7.9 %all_to_all.38.refs_0_ = f32[8,32,128]{2,1,0:T(8,128)S(1)} all-to-all(f32[8,32,128]{2,1,0:T(8,128)S(1)} %get-tuple-element.22), channel_id=1, replica_groups=mesh['yh'=2,'core'=2,'x'=4,'z'=4,'yl'=2] {'z','yl'}, dimensions={0} | all-to-all | bytes 262144 | tf_op jit(solution)/shard_map/all_to_all | solution.py:177
  93.7 14.0 %shard_map.44 = f32[16,32,128]{2,1,0:T(8,128)S(1)} custom-call(f32[8,32,128]{2,1,0:T(8,128)S(1)} %all_to_all.38.refs_0_, bf16[4096,128]{1,0:T(8,128)(2,1)S(1)} %get-tuple-element.15.refs_1_, bf16[4096,128]{1,0:T(8,128)(2,1)S(1)} %get-tuple-element.16.refs_2_, bf16[256,4096]{1,0:T(8,128)(2,1)S(1)} %get-tuple-element.17.refs_3_), custom_call_target="tpu_custom_call" | custom-call | tf_op jit(solution)/shard_map/pallas_call | solution.py:149
  107.7 13.4 %all_to_all.39.parts = f32[16,32,128]{2,1,0:T(8,128)S(1)} all-to-all(f32[16,32,128]{2,1,0:T(8,128)S(1)} %shard_map.44), channel_id=1, replica_groups=mesh['yh'=2,'core'=2,'x'=4,'z'=4,'yl'=2] {'yh','core','x'}, dimensions={0} | all-to-all | bytes 524288 | tf_op jit(solution)/shard_map/all_to_all | solution.py:177
  121.1 14.5 %shard_map.45 = (f32[8,32,128]{2,1,0:T(8,128)}, f32[32,128]{1,0:T(8,128)S(1)}) custom-call(f32[16,32,128]{2,1,0:T(8,128)S(1)} %all_to_all.39.parts, bf16[4096,128]{1,0:T(8,128)(2,1)S(1)} %get-tuple-element.18.main, bf16[4096,128]{1,0:T(8,128)(2,1)S(1)} %get-tuple-element.19.tail, bf16[256,4096]{1,0:T(8,128)(2,1)S(1)} %get-tuple-element.20.rhs, ...), custom_call_target="tpu_custom_call" | custom-call | tf_op jit(solution)/shard_map/pallas_call | solution.py:161
  135.6 3.4 %all-to-all-start.5 = ((f32[8,32,128]{2,1,0:T(8,128)}), f32[8,32,128]{2,1,0:T(8,128)S(1)}, u32[]{:S(2)}, u32[]{:S(2)}) async-start(f32[8,32,128]{2,1,0:T(8,128)} %get-tuple-element.24), calls=%async_computation.5 | async-start | bytes 262144 | tf_op jit(solution)/shard_map/all_to_all | solution.py:177
  139.0 5.5 %all-to-all-done.5.refs_0_ = f32[8,32,128]{2,1,0:T(8,128)S(1)} async-done(((f32[8,32,128]{2,1,0:T(8,128)}), f32[8,32,128]{2,1,0:T(8,128)S(1)}, u32[]{:S(2)}, u32[]{:S(2)}) %all-to-all-start.5) | async-done | bytes 131104 | tf_op jit(solution)/shard_map/all_to_all | solution.py:177
  144.5 0.0 copy-start.1
  144.5 0.6 copy-done.1
  145.1 1.6 %shard_map.46 = f32[4,32,128]{2,1,0:T(8,128)} custom-call(f32[8,32,128]{2,1,0:T(8,128)} %copy-done.1, f32[32,128]{1,0:T(8,128)} %copy-done), custom_call_target="tpu_custom_call" | custom-call | tf_op jit(solution)/shard_map/pallas_call | solution.py:216
  146.7 3.3 %all-to-all-start.6 = ((f32[4,32,128]{2,1,0:T(8,128)}), f32[4,32,128]{2,1,0:T(8,128)S(1)}, u32[]{:S(2)}, u32[]{:S(2)}) async-start(f32[4,32,128]{2,1,0:T(8,128)} %shard_map.46), calls=%async_computation.6 | async-start | bytes 131072 | tf_op jit(solution)/shard_map/all_to_all | solution.py:177
  150.0 0.6 dynamic-slice_bitcast_fusion
  150.6 3.8 %all-to-all-done.6 = f32[4,32,128]{2,1,0:T(8,128)S(1)} async-done(((f32[4,32,128]{2,1,0:T(8,128)}), f32[4,32,128]{2,1,0:T(8,128)S(1)}, u32[]{:S(2)}, u32[]{:S(2)}) %all-to-all-start.6) | async-done | bytes 65568 | tf_op jit(solution)/shard_map/all_to_all | solution.py:177
  154.4 0.6 copy.5
Async XLA Ops:
  0.6 19.9 %copy-start.2 = (f32[64,512]{1,0:T(8,128)S(1)}, f32[64,512]{1,0:T(8,128)}, u32[]{:S(2)}) copy-start(f32[64,512]{1,0:T(8,128)} %param.3) | copy-start | bytes 393220
  41.2 14.0 %copy-start = (f32[32,128]{1,0:T(8,128)}, f32[32,128]{1,0:T(8,128)S(1)}, u32[]{:S(2)}) copy-start(f32[32,128]{1,0:T(8,128)S(1)} %get-tuple-element.25.refs_1_) | copy-start | bytes 49156
  135.6 8.8 %all-to-all-start.5 = ((f32[8,32,128]{2,1,0:T(8,128)}), f32[8,32,128]{2,1,0:T(8,128)S(1)}, u32[]{:S(2)}, u32[]{:S(2)}) async-start(f32[8,32,128]{2,1,0:T(8,128)} %get-tuple-element.24), calls=%async_computation.5 | async-start | bytes 262144 | tf_op jit(solution)/shard_map/all_to_all | solution.py:177
  144.5 0.6 copy-start.1
  146.7 7.7 %all-to-all-start.6 = ((f32[4,32,128]{2,1,0:T(8,128)}), f32[4,32,128]{2,1,0:T(8,128)S(1)}, u32[]{:S(2)}, u32[]{:S(2)}) async-start(f32[4,32,128]{2,1,0:T(8,128)} %shard_map.46), calls=%async_computation.6 | async-start | bytes 131072 | tf_op jit(solution)/shard_map/all_to_all | solution.py:177

commit v2 on v1

v2 whole, which is shorter than its diff:
```python
import math

import jax
import jax.numpy as jnp
from jax import lax
from jax.experimental import pallas as pl
from jax.experimental.pallas import tpu as pltpu
from jax.sharding import Mesh
from jax.sharding import PartitionSpec as P

ITERS = 2
EPS = 0.5
LOG2E = 1.0 / math.log(2.0)
SCALE = LOG2E / EPS

LANES = 128
CHUNK = 256
WIDTH = 256
GROUP = 4
ACC_ROWS = 16
DUAL_LANE = 64
EDGE = 64
SMALLEST = 2.0**-80

f32 = jnp.float32
bf16 = jnp.bfloat16
vmem = pl.BlockSpec(memory_space=pltpu.VMEM)


def split2(value):
    high = value.astype(bf16)
    return high, (value - high.astype(f32)).astype(bf16)


def fold(op, acc, value):
    rows = acc.shape[0]
    for i in range(value.shape[0] // rows):
        acc = op(acc, value[i * rows : (i + 1) * rows])
    return acc


def prepare_side(src, main, tail, rhs, norm, scale):
    blocks, dim, cells = src.shape
    for b in range(blocks):
        value = src[b]
        square = jnp.sum(value * value, axis=0, keepdims=True)
        for q in range(cells // LANES):
            row = b * (cells // LANES) + q
            norm[row : row + 1, :] = square[:, q * LANES : (q + 1) * LANES]
        high, low = split2(value * scale)
        here = pl.ds(b * cells, cells)
        rhs[0:dim, here] = high
        rhs[dim : 2 * dim, here] = low
        rhs[2 * dim : 3 * dim, here] = high
        main[here, :] = jnp.transpose(jnp.concatenate([high, high], axis=0))
        tail[here, :] = jnp.transpose(jnp.concatenate([low, jnp.zeros_like(low)], axis=0))


def prepare_kernel(log_src, x_ref, y_ref, xm, xt, xr, xn, ym, yt, yr, yn, first, before):
    prepare_side(x_ref, xm, xt, xr, xn, 2.0 * SCALE)
    prepare_side(y_ref, ym, yt, yr, yn, 1.0)
    first[0] = log_src + SCALE * yn[...]
    before[...] = log_src - SCALE * xn[...]


def combine(parts, log_count):
    peak = parts[0]
    for i in range(1, parts.shape[0]):
        peak = jnp.maximum(peak, parts[i])
    total = jnp.exp2(parts[0] - peak)
    for i in range(1, parts.shape[0]):
        total = total + jnp.exp2(parts[i] - peak)
    return log_count - (peak + jnp.log2(total))


def split3(value):
    high = value.astype(bf16).astype(f32)
    mid = (value - high).astype(bf16).astype(f32)
    return high, mid, value - high - mid


def placed(parts, row, height, first):
    place = lax.broadcasted_iota(jnp.int32, (height, LANES), 0)
    value = jnp.zeros((height, LANES), f32)
    for i, part in enumerate(parts):
        value = jnp.where(place == first + i, part[row : row + 1], value)
    return value


def pass_kernel(log_count, parts, prev, main, tail, rhs, out, dual_out, full, edge, score):
    length, width = main.shape[0], rhs.shape[1]
    dual = combine(parts, log_count)
    dual_out[...] = dual
    bound = log_count - prev[...]
    duals, bounds = split3(dual), split3(-bound)
    place = lax.broadcasted_iota(jnp.int32, (LANES, LANES), 0)
    for k in range(length // LANES):
        here = pl.ds(k * LANES, LANES)
        rows = placed(duals, k, LANES, DUAL_LANE)
        rows = jnp.where((place >= DUAL_LANE + 3) & (place < DUAL_LANE + 6), 1.0, rows)
        full[here, :] = (tail[here, :].astype(f32) + jnp.transpose(rows)).astype(bf16)
    place = lax.broadcasted_iota(jnp.int32, (EDGE, LANES), 0)
    for k in range(width // LANES):
        rows = jnp.where(place < 3, 1.0, placed(bounds, k, EDGE, 3))
        edge[:, pl.ds(k * LANES, LANES)] = rows.astype(bf16)

    def scores(block, chunk):
        here = pl.ds(chunk * CHUNK, CHUNK)
        lhs = jnp.concatenate([main[here, :], full[here, :]], axis=1)
        cols = pl.ds(pl.multiple_of(block * WIDTH, WIDTH), WIDTH)
        weight = jnp.concatenate([rhs[:, cols], edge[:, cols]], axis=0)
        return jnp.dot(lhs, weight, preferred_element_type=f32)

    def finish(block, value):
        for q in range(WIDTH // LANES):
            row = block * (WIDTH // LANES) + q
            piece = value[:, q * LANES : (q + 1) * LANES][None]
            out[:, pl.ds(row, 1), :] = jnp.broadcast_to(piece, (out.shape[0], 1, LANES))

    chunks, blocks = length // CHUNK, width // WIDTH
    zero = jnp.zeros((ACC_ROWS, WIDTH), f32)

    def step(group, least):
        for t in range(GROUP):
            block = group * GROUP + t
            acc = zero
            for chunk in range(chunks):
                acc = fold(jnp.add, acc, jnp.exp2(scores(block, chunk)))
            total = jnp.sum(acc, axis=0, keepdims=True)
            least = jnp.minimum(least, total)
            finish(block, jnp.log2(total))
        return least

    least = lax.fori_loop(0, blocks // GROUP, step, jnp.full((1, WIDTH), 1.0, f32))

    @pl.when(jnp.min(least) < SMALLEST)
    def _():
        def exact(block, carry):
            peak = jnp.full((ACC_ROWS, WIDTH), -jnp.inf, f32)
            for chunk in range(chunks):
                value = scores(block, chunk)
                score[pl.ds(chunk * CHUNK, CHUNK), :] = value
                peak = fold(jnp.maximum, peak, value)
            top = jnp.max(peak, axis=0, keepdims=True)
            acc = zero
            for chunk in range(chunks):
                acc = fold(jnp.add, acc, jnp.exp2(score[pl.ds(chunk * CHUNK, CHUNK), :] - top))
            finish(block, top + jnp.log2(jnp.sum(acc, axis=0, keepdims=True)))
            return carry

        lax.fori_loop(0, blocks, exact, 0)

    for i in range(out.shape[0]):
        out[i] = out[i] + bound


def final_kernel(log_src, parts, yn, dual, xn, col_out, row_out):
    value = combine(parts, log_src) * (1.0 / SCALE) + yn[...]
    for i in range(col_out.shape[0]):
        col_out[i] = value
    row_out[...] = dual[...] * (1.0 / SCALE) + xn[...]


def params(mib):
    return pltpu.CompilerParams(vmem_limit_bytes=mib * 2**20)


def lse_pass(log_count, parts, prev, main, tail, rhs, copies):
    length, width = main.shape[0], rhs.shape[1]
    return pl.pallas_call(
        lambda *refs: pass_kernel(log_count, *refs),
        out_shape=(
            jax.ShapeDtypeStruct((copies, width // LANES, LANES), f32),
            jax.ShapeDtypeStruct((length // LANES, LANES), f32),
        ),
        in_specs=[vmem] * 5,
        out_specs=(vmem, vmem),
        scratch_shapes=[
            pltpu.VMEM((length, LANES), bf16),
            pltpu.VMEM((EDGE, width), bf16),
            pltpu.VMEM((length, WIDTH), f32),
        ],
        compiler_params=params(20),
    )(parts, prev, main, tail, rhs)


def gathered(value, axes):
    copies = jnp.broadcast_to(value[None], (lax.axis_size(axes),) + value.shape)
    return lax.all_to_all(copies, axes, 0, 0, tiled=True)


def exchanged(parts, axes):
    return lax.all_to_all(parts, axes, 0, 0, tiled=True)


ROW_GATHER = "x"
COL_GATHER = ("z", "yl")
ROW_PEERS = ("yh", "core", "x")
COL_PEERS = ("z", "yl")


def on_device(x_feat, y_feat):
    xg = gathered(x_feat, ROW_GATHER)
    yg = gathered(y_feat, COL_GATHER)
    rows, cols = xg.shape[0] * xg.shape[2], yg.shape[0] * yg.shape[2]
    row_peers, col_peers = lax.axis_size(ROW_PEERS), lax.axis_size(COL_PEERS)
    log_tgt = math.log2(cols * row_peers)
    log_src = math.log2(rows * col_peers)

    def side(cells):
        return [
            jax.ShapeDtypeStruct((cells, LANES), bf16),
            jax.ShapeDtypeStruct((cells, LANES), bf16),
            jax.ShapeDtypeStruct((3 * x_feat.shape[0], cells), bf16),
            jax.ShapeDtypeStruct((cells // LANES, LANES), f32),
        ]

    xm, xt, xr, xn, ym, yt, yr, yn, parts, before = pl.pallas_call(
        lambda *refs: prepare_kernel(log_src, *refs),
        out_shape=side(rows)
        + side(cols)
        + [
            jax.ShapeDtypeStruct((1, cols // LANES, LANES), f32),
            jax.ShapeDtypeStruct((rows // LANES, LANES), f32),
        ],
        in_specs=[vmem] * 2,
        out_specs=[vmem] * 10,
        compiler_params=params(20),
    )(xg, yg)
    dual_x = before
    for iteration in range(ITERS):
        sums, dual_y = lse_pass(log_src, parts, dual_x, ym, yt, xr, row_peers)
        parts = exchanged(sums, ROW_PEERS)
        sums, dual_x = lse_pass(log_tgt, parts, dual_y, xm, xt, yr, col_peers)
        parts = exchanged(sums, COL_PEERS)
    spread = lax.axis_size(ROW_GATHER)
    dual_col, dual_row = pl.pallas_call(
        lambda *refs: final_kernel(log_src, *refs),
        out_shape=(
            jax.ShapeDtypeStruct((spread, cols // LANES, LANES), f32),
            jax.ShapeDtypeStruct((rows // LANES, LANES), f32),
        ),
        in_specs=[vmem] * 4,
        out_specs=(vmem, vmem),
    )(parts, yn, dual_x, xn)
    own = x_feat.shape[1] // LANES
    dual_row = lax.dynamic_slice_in_dim(dual_row, lax.axis_index(ROW_GATHER) * own, own, 0)
    dual_col = exchanged(dual_col, ROW_GATHER)
    return dual_row.reshape(-1), dual_col.reshape(-1)


def solution(mesh):
    fine = Mesh(mesh.devices.reshape(2, 2, 4, 4, 2), ("yh", "core", "x", "z", "yl"))
    dev = ("x", "z", "yl")
    in_specs = (P(None, dev), P(None, ("yh", "core") + dev))
    out_specs = (P(dev), P(("yh", "core")))
    return jax.shard_map(
        on_device, mesh=fine, in_specs=in_specs, out_specs=out_specs, check_vma=False
    )
```

time: 157 us -> 225 us (1.43)
  the two profiles are of different devices: /device:TPU:1 before, /device:TPU:17 now
where the time goes in v2:
time: 225 us; the launch traced here: 223 us
  Pallas kernels  129 us (57%)
  blocking collectives  73.2 us (33%)
  waiting for transfers between devices  8.63 us (4%)
  starting transfers between devices  6.65 us (3%)
  local copies, waits for them, and re-layouts  4.98 us (2%)
    pallas_call x4, Pallas kernels, lse_pass(): pl.pallas_call(lambda *refs: pass_kernel(log_count, *refs), out_shape=(ja...  126 us
    all_to_all x2, blocking collectives, gathered(): return lax.all_to_all(copies, axes, 0, 0, tiled=True)  36.9 us
    all_to_all x3, blocking collectives, exchanged(): return lax.all_to_all(parts, axes, 0, 0, tiled=True)  36.2 us
    all_to_all x2, waiting for transfers between devices, exchanged(): return lax.all_to_all(parts, axes, 0, 0, tiled=True)  8.63 us
    all_to_all x2, starting transfers between devices, exchanged(): return lax.all_to_all(parts, axes, 0, 0, tiled=True)  6.65 us
  transfers between devices with their start and end apart: 2, of which 2 were waited for; matrix products, arithmetic and copies ran while one was open for 1% of the time, Pallas kernels for 0%

profile of v2, /device:TPU:17, one launch (start us, length us, event | category | flops | bytes accessed | tf_op | source)
XLA Modules:
  0.0 223.0 jit_solution(10612191930086732010)
XLA Ops:
  0.6 0.0 copy-start.4
  0.6 1.1 broadcast_in_dim.4
  1.7 18.0 %all_to_all.35.refs_0_ = f32[4,64,1024]{2,1,0:T(8,128)S(1)} all-to-all(f32[4,64,1024]{2,1,0:T(8,128)S(1)} %broadcast_in_dim.4), channel_id=1, replica_groups=mesh['yh'=2,'core'=2,'x'=4,'z'=4,'yl'=2] {'x'}, dimensions={0} | all-to-all | bytes 2097152 | tf_op jit(solution)/shard_map/all_to_all | solution.py:189
  19.7 0.0 copy-done.4
  19.7 0.1 broadcast_in_dim.5
  19.9 18.9 %all_to_all.36.refs_1_ = f32[8,64,512]{2,1,0:T(8,128)S(1)} all-to-all(f32[8,64,512]{2,1,0:T(8,128)S(1)} %broadcast_in_dim.5), channel_id=1, replica_groups=mesh['yh'=2,'core'=2,'x'=4,'z'=4,'yl'=2] {'z','yl'}, dimensions={0} | all-to-all | bytes 2097152 | tf_op jit(solution)/shard_map/all_to_all | solution.py:189
  38.8 1.2 shard_map.41
  40.1 0.0 copy-start
  40.1 0.6 copy-done
  40.7 0.0 copy-start.1
  40.7 31.5 %shard_map.42 = (f32[16,32,128]{2,1,0:T(8,128)S(1)}, f32[32,128]{1,0:T(8,128)S(1)}) custom-call(f32[1,32,128]{2,1,0:T(8,128)S(1)} %get-tuple-element.22.refs_0_, f32[32,128]{1,0:T(8,128)S(1)} %get-tuple-element.23.refs_1_, bf16[4096,128]{1,0:T(8,128)(2,1)S(1)} %get-tuple-element.24.refs_2_, bf16[4096,128]{1,0:T(8,128)(2,1)S(1)} %get-tuple-element.25.refs_3_, ...), custom_call_target="tpu_custom_call" | custom-call | tf_op jit(solution)/shard_map/pallas_call | solution.py:170
  72.1 0.0 copy-done.1
  72.1 14.9 %all_to_all.37.refs_0_ = f32[16,32,128]{2,1,0:T(8,128)S(1)} all-to-all(f32[16,32,128]{2,1,0:T(8,128)S(1)} %get-tuple-element.27), channel_id=1, replica_groups=mesh['yh'=2,'core'=2,'x'=4,'z'=4,'yl'=2] {'yh','core','x'}, dimensions={0} | all-to-all | bytes 524288 | tf_op jit(solution)/shard_map/all_to_all | solution.py:193
  87.0 31.2 %shard_map.43 = (f32[8,32,128]{2,1,0:T(8,128)S(1)}, f32[32,128]{1,0:T(8,128)S(1)}) custom-call(f32[16,32,128]{2,1,0:T(8,128)S(1)} %all_to_all.37.refs_0_, f32[32,128]{1,0:T(8,128)S(1)} %get-tuple-element.28.refs_1_, bf16[4096,128]{1,0:T(8,128)(2,1)S(1)} %get-tuple-element.29.refs_2_, bf16[4096,128]{1,0:T(8,128)(2,1)S(1)} %get-tuple-element.30.refs_3_, ...), custom_call_target="tpu_custom_call" | custom-call | tf_op jit(solution)/shard_map/pallas_call | solution.py:170
  118.2 8.0 %all_to_all.38.refs_0_ = f32[8,32,128]{2,1,0:T(8,128)S(1)} all-to-all(f32[8,32,128]{2,1,0:T(8,128)S(1)} %get-tuple-element.32), channel_id=1, replica_groups=mesh['yh'=2,'core'=2,'x'=4,'z'=4,'yl'=2] {'z','yl'}, dimensions={0} | all-to-all | bytes 262144 | tf_op jit(solution)/shard_map/all_to_all | solution.py:193
  126.2 31.5 %shard_map.44 = (f32[16,32,128]{2,1,0:T(8,128)S(1)}, f32[32,128]{1,0:T(8,128)S(1)}) custom-call(f32[8,32,128]{2,1,0:T(8,128)S(1)} %all_to_all.38.refs_0_, f32[32,128]{1,0:T(8,128)S(1)} %get-tuple-element.33.refs_1_, bf16[4096,128]{1,0:T(8,128)(2,1)S(1)} %get-tuple-element.24.refs_2_, bf16[4096,128]{1,0:T(8,128)(2,1)S(1)} %get-tuple-element.25.refs_3_, ...), custom_call_target="tpu_custom_call" | custom-call | tf_op jit(solution)/shard_map/pallas_call | solution.py:170
  157.7 13.4 %all_to_all.39.refs_0_ = f32[16,32,128]{2,1,0:T(8,128)S(1)} all-to-all(f32[16,32,128]{2,1,0:T(8,128)S(1)} %get-tuple-element.34), channel_id=1, replica_groups=mesh['yh'=2,'core'=2,'x'=4,'z'=4,'yl'=2] {'yh','core','x'}, dimensions={0} | all-to-all | bytes 524288 | tf_op jit(solution)/shard_map/all_to_all | solution.py:193
  171.1 31.9 %shard_map.45 = (f32[8,32,128]{2,1,0:T(8,128)}, f32[32,128]{1,0:T(8,128)S(1)}) custom-call(f32[16,32,128]{2,1,0:T(8,128)S(1)} %all_to_all.39.refs_0_, f32[32,128]{1,0:T(8,128)S(1)} %get-tuple-element.35.refs_1_, bf16[4096,128]{1,0:T(8,128)(2,1)S(1)} %get-tuple-element.29.refs_2_, bf16[4096,128]{1,0:T(8,128)(2,1)S(1)} %get-tuple-element.30.refs_3_, ...), custom_call_target="tpu_custom_call" | custom-call | tf_op jit(solution)/shard_map/pallas_call | solution.py:170
  203.0 0.0 copy-start.2
  203.0 0.6 copy-done.2
  203.6 3.4 %all-to-all-start.5 = ((f32[8,32,128]{2,1,0:T(8,128)}), f32[8,32,128]{2,1,0:T(8,128)S(1)}, u32[]{:S(2)}, u32[]{:S(2)}) async-start(f32[8,32,128]{2,1,0:T(8,128)} %get-tuple-element.36), calls=%async_computation.5 | async-start | bytes 262144 | tf_op jit(solution)/shard_map/all_to_all | solution.py:193
  206.9 5.5 %all-to-all-done.5.refs_0_ = f32[8,32,128]{2,1,0:T(8,128)S(1)} async-done(((f32[8,32,128]{2,1,0:T(8,128)}), f32[8,32,128]{2,1,0:T(8,128)S(1)}, u32[]{:S(2)}, u32[]{:S(2)}) %all-to-all-start.5) | async-done | bytes 131104 | tf_op jit(solution)/shard_map/all_to_all | solution.py:193
  212.4 0.0 copy-start.3
  212.4 0.6 copy-done.3
  213.1 1.6 shard_map.46
  214.7 3.3 %all-to-all-start.6 = ((f32[4,32,128]{2,1,0:T(8,128)}), f32[4,32,128]{2,1,0:T(8,128)S(1)}, u32[]{:S(2)}, u32[]{:S(2)}) async-start(f32[4,32,128]{2,1,0:T(8,128)} %get-tuple-element.41), calls=%async_computation.6 | async-start | bytes 131072 | tf_op jit(solution)/shard_map/all_to_all | solution.py:193
  218.0 1.3 dynamic-slice_bitcast_fusion
  219.2 3.2 %all-to-all-done.6 = f32[4,32,128]{2,1,0:T(8,128)S(1)} async-done(((f32[4,32,128]{2,1,0:T(8,128)}), f32[4,32,128]{2,1,0:T(8,128)S(1)}, u32[]{:S(2)}, u32[]{:S(2)}) %all-to-all-start.6) | async-done | bytes 65568 | tf_op jit(solution)/shard_map/all_to_all | solution.py:193
  222.4 0.6 copy.5
Async XLA Ops:
  0.6 19.1 %copy-start.4 = (f32[64,512]{1,0:T(8,128)S(1)}, f32[64,512]{1,0:T(8,128)}, u32[]{:S(2)}) copy-start(f32[64,512]{1,0:T(8,128)} %param.3) | copy-start | bytes 393220
  40.1 0.6 copy-start
  40.7 31.5 %copy-start.1 = (f32[32,128]{1,0:T(8,128)}, f32[32,128]{1,0:T(8,128)S(1)}, u32[]{:S(2)}) copy-start(f32[32,128]{1,0:T(8,128)S(1)} %get-tuple-element.37.refs_1_) | copy-start | bytes 49156
  203.0 0.6 copy-start.2
  203.6 8.8 %all-to-all-start.5 = ((f32[8,32,128]{2,1,0:T(8,128)}), f32[8,32,128]{2,1,0:T(8,128)S(1)}, u32[]{:S(2)}, u32[]{:S(2)}) async-start(f32[8,32,128]{2,1,0:T(8,128)} %get-tuple-element.36), calls=%async_computation.5 | async-start | bytes 262144 | tf_op jit(solution)/shard_map/all_to_all | solution.py:193
  212.4 0.7 copy-start.3
  214.7 7.7 %all-to-all-start.6 = ((f32[4,32,128]{2,1,0:T(8,128)}), f32[4,32,128]{2,1,0:T(8,128)S(1)}, u32[]{:S(2)}, u32[]{:S(2)}) async-start(f32[4,32,128]{2,1,0:T(8,128)} %get-tuple-element.41), calls=%async_computation.6 | async-start | bytes 131072 | tf_op jit(solution)/shard_map/all_to_all | solution.py:193

commit v3 on v2

--- a/solution.py
+++ b/solution.py
@@ -39,26 +39,28 @@
     return acc
 
 
-def prepare_side(src, main, tail, rhs, norm, scale):
-    blocks, dim, cells = src.shape
-    for b in range(blocks):
-        value = src[b]
-        square = jnp.sum(value * value, axis=0, keepdims=True)
-        for q in range(cells // LANES):
-            row = b * (cells // LANES) + q
-            norm[row : row + 1, :] = square[:, q * LANES : (q + 1) * LANES]
-        high, low = split2(value * scale)
-        here = pl.ds(b * cells, cells)
-        rhs[0:dim, here] = high
-        rhs[dim : 2 * dim, here] = low
-        rhs[2 * dim : 3 * dim, here] = high
-        main[here, :] = jnp.transpose(jnp.concatenate([high, high], axis=0))
-        tail[here, :] = jnp.transpose(jnp.concatenate([low, jnp.zeros_like(low)], axis=0))
-
-
-def prepare_kernel(log_src, x_ref, y_ref, xm, xt, xr, xn, ym, yt, yr, yn, first, before):
-    prepare_side(x_ref, xm, xt, xr, xn, 2.0 * SCALE)
-    prepare_side(y_ref, ym, yt, yr, yn, 1.0)
+def prepare_block(value, at, main, tail, rhs, norm, scale):
+    dim, cells = value.shape
+    rows = cells // LANES
+    square = jnp.sum(value * value, axis=0, keepdims=True)
+    for q in range(rows):
+        norm[pl.ds(at * rows + q, 1), :] = square[:, q * LANES : (q + 1) * LANES]
+    high, low = split2(value * scale)
+    here = pl.ds(pl.multiple_of(at * cells, cells), cells)
+    rhs[0:dim, here] = high
+    rhs[dim : 2 * dim, here] = low
+    rhs[2 * dim : 3 * dim, here] = high
+    main[here, :] = jnp.transpose(jnp.concatenate([high, high], axis=0))
+    tail[here, :] = jnp.transpose(jnp.concatenate([low, jnp.zeros_like(low)], axis=0))
+
+
+def prepare_kernel(log_src, index, *refs):
+    xs, (y_ref, xm, xt, xr, xn, ym, yt, yr, yn, first, before) = refs[:-11], refs[-11:]
+    for shift, x_ref in enumerate(xs):
+        at = lax.rem(index[0] + len(xs) - shift, len(xs))
+        prepare_block(x_ref[...], at, xm, xt, xr, xn, 2.0 * SCALE)
+    for at in range(y_ref.shape[0]):
+        prepare_block(y_ref[at], at, ym, yt, yr, yn, 1.0)
     first[0] = log_src + SCALE * yn[...]
     before[...] = log_src - SCALE * xn[...]
 
@@ -200,9 +202,13 @@
 
 
 def on_device(x_feat, y_feat):
-    xg = gathered(x_feat, ROW_GATHER)
+    ring = lax.axis_size(ROW_GATHER)
+    blocks = [x_feat]
+    for shift in range(1, ring):
+        pairs = [(i, (i + shift) % ring) for i in range(ring)]
+        blocks.append(lax.ppermute(x_feat, ROW_GATHER, pairs))
     yg = gathered(y_feat, COL_GATHER)
-    rows, cols = xg.shape[0] * xg.shape[2], yg.shape[0] * yg.shape[2]
+    rows, cols = ring * x_feat.shape[1], yg.shape[0] * yg.shape[2]
     row_peers, col_peers = lax.axis_size(ROW_PEERS), lax.axis_size(COL_PEERS)
     log_tgt = math.log2(cols * row_peers)
     log_src = math.log2(rows * col_peers)
@@ -223,21 +229,20 @@
             jax.ShapeDtypeStruct((1, cols // LANES, LANES), f32),
             jax.ShapeDtypeStruct((rows // LANES, LANES), f32),
         ],
-        in_specs=[vmem] * 2,
+        in_specs=[pl.BlockSpec(memory_space=pltpu.SMEM)] + [vmem] * (ring + 1),
         out_specs=[vmem] * 10,
         compiler_params=params(20),
-    )(xg, yg)
+    )(lax.axis_index(ROW_GATHER).reshape(1), *blocks, yg)
     dual_x = before
     for iteration in range(ITERS):
         sums, dual_y = lse_pass(log_src, parts, dual_x, ym, yt, xr, row_peers)
         parts = exchanged(sums, ROW_PEERS)
         sums, dual_x = lse_pass(log_tgt, parts, dual_y, xm, xt, yr, col_peers)
         parts = exchanged(sums, COL_PEERS)
-    spread = lax.axis_size(ROW_GATHER)
     dual_col, dual_row = pl.pallas_call(
         lambda *refs: final_kernel(log_src, *refs),
         out_shape=(
-            jax.ShapeDtypeStruct((spread, cols // LANES, LANES), f32),
+            jax.ShapeDtypeStruct((ring, cols // LANES, LANES), f32),
             jax.ShapeDtypeStruct((rows // LANES, LANES), f32),
         ),
         in_specs=[vmem] * 4,

time: 225 us -> 213 us (0.947)
  the two profiles are of different devices: /device:TPU:17 before, /device:TPU:16 now
where the time goes in v3:
time: 213 us; the launch traced here: 211 us
  Pallas kernels  108 us (51%)
  starting transfers between devices  37.8 us (18%)
  blocking collectives  37.2 us (17%)
  waiting for transfers between devices  21 us (10%)
  local copies, waits for them, and re-layouts  5.8 us (3%)
    pallas_call x4, Pallas kernels, lse_pass(): pl.pallas_call(lambda *refs: pass_kernel(log_count, *refs), out_shape=(ja...  105 us
    all_to_all x3, blocking collectives, exchanged(): return lax.all_to_all(parts, axes, 0, 0, tiled=True)  37.2 us
    all_to_all x2, starting transfers between devices, exchanged(): return lax.all_to_all(parts, axes, 0, 0, tiled=True)  26.1 us
    all_to_all x2, waiting for transfers between devices, exchanged(): return lax.all_to_all(parts, axes, 0, 0, tiled=True)  11 us
    ppermute x3, waiting for transfers between devices, on_device(): blocks.append(lax.ppermute(x_feat, ROW_GATHER, pairs))  9.92 us
    all_to_all x1, starting transfers between devices, gathered(): return lax.all_to_all(copies, axes, 0, 0, tiled=True)  6.03 us
    ppermute x3, starting transfers between devices, on_device(): blocks.append(lax.ppermute(x_feat, ROW_GATHER, pairs))  5.72 us
  transfers between devices with their start and end apart: 6, of which 4 were waited for; matrix products, arithmetic and copies ran while one was open for 1% of the time, Pallas kernels for 0%

profile of v3, /device:TPU:16, one launch (start us, length us, event | category | flops | bytes accessed | tf_op | source)
XLA Modules:
  0.0 210.6 jit_solution(9997884823729852258)
XLA Ops:
  0.6 0.0 copy-start
  0.6 2.1 broadcast_in_dim.2
  2.7 6.0 %all-to-all-start = ((f32[8,64,512]{2,1,0:T(8,128)}), f32[8,64,512]{2,1,0:T(8,128)S(1)}, u32[]{:S(2)}, u32[]{:S(2)}) async-start(f32[8,64,512]{2,1,0:T(8,128)} %broadcast_in_dim.2), calls=%async_computation | async-start | bytes 2097152 | tf_op jit(solution)/shard_map/all_to_all | solution.py:191
  8.7 0.0 copy-done
  8.7 1.6 collective-permute-start
  10.3 2.7 %collective-permute-start.1 = (f32[64,1024]{1,0:T(8,128)S(1)}, f32[64,1024]{1,0:T(8,128)S(1)}, u32[]{:S(2)}, u32[]{:S(2)}) collective-permute-start(f32[64,1024]{1,0:T(8,128)S(1)} %copy-done), channel_id=1, source_target_pairs={{0,16},{8,24},{16,0},{24,8},{1,17},{9,25},{17,1},{25,9},{2,18},{10... | collective-permute-start | bytes 786440 | tf_op jit(solution)/shard_map/ppermute | solution.py:209
  13.0 1.4 collective-permute-start.2
  14.5 3.8 %collective-permute-done.refs_2_ = f32[64,1024]{1,0:T(8,128)S(1)} collective-permute-done((f32[64,1024]{1,0:T(8,128)S(1)}, f32[64,1024]{1,0:T(8,128)S(1)}, u32[]{:S(2)}, u32[]{:S(2)}) %collective-permute-start) | collective-permute-done | bytes 262176 | tf_op jit(solution)/shard_map/ppermute | solution.py:209
  18.3 6.1 %collective-permute-done.1.refs_3_ = f32[64,1024]{1,0:T(8,128)S(1)} collective-permute-done((f32[64,1024]{1,0:T(8,128)S(1)}, f32[64,1024]{1,0:T(8,128)S(1)}, u32[]{:S(2)}, u32[]{:S(2)}) %collective-permute-start.1) | collective-permute-done | bytes 262176 | tf_op jit(solution)/shard_map/ppermute | solution.py:209
  24.4 0.0 collective-permute-done.2.refs_4_
  24.4 0.0 all-to-all-done.refs_5_
  24.4 1.2 shard_map.41
  25.7 0.0 copy-start.1
  25.7 0.6 copy-done.1
  26.3 0.0 copy-start.2
  26.3 31.5 %shard_map.42 = (f32[16,32,128]{2,1,0:T(8,128)S(1)}, f32[32,128]{1,0:T(8,128)S(1)}) custom-call(f32[1,32,128]{2,1,0:T(8,128)S(1)} %get-tuple-element.22.refs_0_, f32[32,128]{1,0:T(8,128)S(1)} %get-tuple-element.23.refs_1_, bf16[4096,128]{1,0:T(8,128)(2,1)S(1)} %get-tuple-element.24.refs_2_, bf16[4096,128]{1,0:T(8,128)(2,1)S(1)} %get-tuple-element.25.refs_3_, ...), custom_call_target="tpu_custom_call" | custom-call | tf_op jit(solution)/shard_map/pallas_call | solution.py:172
  57.7 0.0 copy-done.2
  57.8 13.6 %all_to_all.30.refs_0_ = f32[16,32,128]{2,1,0:T(8,128)S(1)} all-to-all(f32[16,32,128]{2,1,0:T(8,128)S(1)} %get-tuple-element.27), channel_id=1, replica_groups=mesh['yh'=2,'core'=2,'x'=4,'z'=4,'yl'=2] {'yh','core','x'}, dimensions={0} | all-to-all | bytes 524288 | tf_op jit(solution)/shard_map/all_to_all | solution.py:195
  71.3 31.2 %shard_map.43 = (f32[8,32,128]{2,1,0:T(8,128)S(1)}, f32[32,128]{1,0:T(8,128)S(1)}) custom-call(f32[16,32,128]{2,1,0:T(8,128)S(1)} %all_to_all.30.refs_0_, f32[32,128]{1,0:T(8,128)S(1)} %get-tuple-element.28.refs_1_, bf16[4096,128]{1,0:T(8,128)(2,1)S(1)} %get-tuple-element.29.refs_2_, bf16[4096,128]{1,0:T(8,128)(2,1)S(1)} %get-tuple-element.30.refs_3_, ...), custom_call_target="tpu_custom_call" | custom-call | tf_op jit(solution)/shard_map/pallas_call | solution.py:172
  102.6 11.4 %all_to_all.31.refs_0_ = f32[8,32,128]{2,1,0:T(8,128)S(1)} all-to-all(f32[8,32,128]{2,1,0:T(8,128)S(1)} %get-tuple-element.32), channel_id=1, replica_groups=mesh['yh'=2,'core'=2,'x'=4,'z'=4,'yl'=2] {'z','yl'}, dimensions={0} | all-to-all | bytes 262144 | tf_op jit(solution)/shard_map/all_to_all | solution.py:195
  114.0 31.5 %shard_map.44 = (f32[16,32,128]{2,1,0:T(8,128)S(1)}, f32[32,128]{1,0:T(8,128)S(1)}) custom-call(f32[8,32,128]{2,1,0:T(8,128)S(1)} %all_to_all.31.refs_0_, f32[32,128]{1,0:T(8,128)S(1)} %get-tuple-element.33.refs_1_, bf16[4096,128]{1,0:T(8,128)(2,1)S(1)} %get-tuple-element.24.refs_2_, bf16[4096,128]{1,0:T(8,128)(2,1)S(1)} %get-tuple-element.25.refs_3_, ...), custom_call_target="tpu_custom_call" | custom-call | tf_op jit(solution)/shard_map/pallas_call | solution.py:172
  145.5 12.2 %all_to_all.32.refs_0_ = f32[16,32,128]{2,1,0:T(8,128)S(1)} all-to-all(f32[16,32,128]{2,1,0:T(8,128)S(1)} %get-tuple-element.34), channel_id=1, replica_groups=mesh['yh'=2,'core'=2,'x'=4,'z'=4,'yl'=2] {'yh','core','x'}, dimensions={0} | all-to-all | bytes 524288 | tf_op jit(solution)/shard_map/all_to_all | solution.py:195
  157.7 11.0 %shard_map.45 = (f32[8,32,128]{2,1,0:T(8,128)}, f32[32,128]{1,0:T(8,128)S(1)}) custom-call(f32[16,32,128]{2,1,0:T(8,128)S(1)} %all_to_all.32.refs_0_, f32[32,128]{1,0:T(8,128)S(1)} %get-tuple-element.35.refs_1_, bf16[4096,128]{1,0:T(8,128)(2,1)S(1)} %get-tuple-element.29.refs_2_, bf16[4096,128]{1,0:T(8,128)(2,1)S(1)} %get-tuple-element.30.refs_3_, ...), custom_call_target="tpu_custom_call" | custom-call | tf_op jit(solution)/shard_map/pallas_call | solution.py:172
  168.7 0.6 copy-done.3
  169.3 3.4 %all-to-all-start.4 = ((f32[8,32,128]{2,1,0:T(8,128)}), f32[8,32,128]{2,1,0:T(8,128)S(1)}, u32[]{:S(2)}, u32[]{:S(2)}) async-start(f32[8,32,128]{2,1,0:T(8,128)} %get-tuple-element.36), calls=%async_computation.4 | async-start | bytes 262144 | tf_op jit(solution)/shard_map/all_to_all | solution.py:195
  172.7 6.6 %all-to-all-done.4.refs_0_ = f32[8,32,128]{2,1,0:T(8,128)S(1)} async-done(((f32[8,32,128]{2,1,0:T(8,128)}), f32[8,32,128]{2,1,0:T(8,128)S(1)}, u32[]{:S(2)}, u32[]{:S(2)}) %all-to-all-start.4) | async-done | bytes 131104 | tf_op jit(solution)/shard_map/all_to_all | solution.py:195
  179.3 0.7 copy-done.4
  180.0 1.6 shard_map.46
  181.6 22.7 %all-to-all-start.5 = ((f32[4,32,128]{2,1,0:T(8,128)}), f32[4,32,128]{2,1,0:T(8,128)S(1)}, u32[]{:S(2)}, u32[]{:S(2)}) async-start(f32[4,32,128]{2,1,0:T(8,128)} %get-tuple-element.41), calls=%async_computation.5 | async-start | bytes 131072 | tf_op jit(solution)/shard_map/all_to_all | solution.py:195
  204.3 1.3 dynamic-slice_bitcast_fusion
  205.6 4.4 %all-to-all-done.5 = f32[4,32,128]{2,1,0:T(8,128)S(1)} async-done(((f32[4,32,128]{2,1,0:T(8,128)}), f32[4,32,128]{2,1,0:T(8,128)S(1)}, u32[]{:S(2)}, u32[]{:S(2)}) %all-to-all-start.5) | async-done | bytes 65568 | tf_op jit(solution)/shard_map/all_to_all | solution.py:195
  209.9 0.6 copy.5
  (2 shorter events, 0.0 us)
Async XLA Ops:
  0.6 8.1 %copy-start = (f32[64,1024]{1,0:T(8,128)S(1)}, f32[64,1024]{1,0:T(8,128)}, u32[]{:S(2)}) copy-start(f32[64,1024]{1,0:T(8,128)} %refs_1_.1) | copy-start | bytes 786436
  2.7 21.7 %all-to-all-start = ((f32[8,64,512]{2,1,0:T(8,128)}), f32[8,64,512]{2,1,0:T(8,128)S(1)}, u32[]{:S(2)}, u32[]{:S(2)}) async-start(f32[8,64,512]{2,1,0:T(8,128)} %broadcast_in_dim.2), calls=%async_computation | async-start | bytes 2097152 | tf_op jit(solution)/shard_map/all_to_all | solution.py:191
  8.7 9.5 %collective-permute-start = (f32[64,1024]{1,0:T(8,128)S(1)}, f32[64,1024]{1,0:T(8,128)S(1)}, u32[]{:S(2)}, u32[]{:S(2)}) collective-permute-start(f32[64,1024]{1,0:T(8,128)S(1)} %copy-done), channel_id=1, source_target_pairs={{0,8},{8,16},{16,24},{24,0},{1,9},{9,17},{17,25},{25,1},{2,10},{10... | collective-permute-start | bytes 786440 | tf_op jit(solution)/shard_map/ppermute | solution.py:209
  10.3 14.1 %collective-permute-start.1 = (f32[64,1024]{1,0:T(8,128)S(1)}, f32[64,1024]{1,0:T(8,128)S(1)}, u32[]{:S(2)}, u32[]{:S(2)}) collective-permute-start(f32[64,1024]{1,0:T(8,128)S(1)} %copy-done), channel_id=1, source_target_pairs={{0,16},{8,24},{16,0},{24,8},{1,17},{9,25},{17,1},{25,9},{2,18},{10... | collective-permute-start | bytes 786440 | tf_op jit(solution)/shard_map/ppermute | solution.py:209
  13.0 11.4 %collective-permute-start.2 = (f32[64,1024]{1,0:T(8,128)S(1)}, f32[64,1024]{1,0:T(8,128)S(1)}, u32[]{:S(2)}, u32[]{:S(2)}) collective-permute-start(f32[64,1024]{1,0:T(8,128)S(1)} %copy-done), channel_id=1, source_target_pairs={{0,24},{8,0},{16,8},{24,16},{1,25},{9,1},{17,9},{25,17},{2,26},{10... | collective-permute-start | bytes 786440 | tf_op jit(solution)/shard_map/ppermute | solution.py:209
  25.7 0.6 copy-start.1
  26.3 31.5 %copy-start.2 = (f32[32,128]{1,0:T(8,128)}, f32[32,128]{1,0:T(8,128)S(1)}, u32[]{:S(2)}) copy-start(f32[32,128]{1,0:T(8,128)S(1)} %get-tuple-element.37.refs_1_) | copy-start | bytes 49156
  168.7 0.6 copy-start.3
  169.3 10.0 %all-to-all-start.4 = ((f32[8,32,128]{2,1,0:T(8,128)}), f32[8,32,128]{2,1,0:T(8,128)S(1)}, u32[]{:S(2)}, u32[]{:S(2)}) async-start(f32[8,32,128]{2,1,0:T(8,128)} %get-tuple-element.36), calls=%async_computation.4 | async-start | bytes 262144 | tf_op jit(solution)/shard_map/all_to_all | solution.py:195
  179.3 0.7 copy-start.4
  181.6 28.3 %all-to-all-start.5 = ((f32[4,32,128]{2,1,0:T(8,128)}), f32[4,32,128]{2,1,0:T(8,128)S(1)}, u32[]{:S(2)}, u32[]{:S(2)}) async-start(f32[4,32,128]{2,1,0:T(8,128)} %get-tuple-element.41), calls=%async_computation.5 | async-start | bytes 131072 | tf_op jit(solution)/shard_map/all_to_all | solution.py:195

commit v4 on v3

--- a/solution.py
+++ b/solution.py
@@ -25,6 +25,7 @@
 f32 = jnp.float32
 bf16 = jnp.bfloat16
 vmem = pl.BlockSpec(memory_space=pltpu.VMEM)
+smem = pl.BlockSpec(memory_space=pltpu.SMEM)
 
 
 def split2(value):
@@ -89,7 +90,7 @@
     return value
 
 
-def pass_kernel(log_count, parts, prev, main, tail, rhs, out, dual_out, full, edge, score):
+def pass_kernel(log_count, parts, prev, norm, main, tail, rhs, out, dual_out, full, edge, score):
     length, width = main.shape[0], rhs.shape[1]
     dual = combine(parts, log_count)
     dual_out[...] = dual
@@ -152,38 +153,48 @@
 
         lax.fori_loop(0, blocks, exact, 0)
 
+    offset = bound if norm is None else bound - SCALE * norm[...]
     for i in range(out.shape[0]):
-        out[i] = out[i] + bound
-
-
-def final_kernel(log_src, parts, yn, dual, xn, col_out, row_out):
-    value = combine(parts, log_src) * (1.0 / SCALE) + yn[...]
-    for i in range(col_out.shape[0]):
-        col_out[i] = value
-    row_out[...] = dual[...] * (1.0 / SCALE) + xn[...]
+        out[i] = out[i] + offset
+
+
+def final_kernel(log_src, index, parts, dual, xn, col_out, row_out):
+    blocks = col_out.shape[0]
+    peers = parts.shape[0] // blocks
+    for block in range(blocks):
+        col_out[block] = combine(parts[block * peers : (block + 1) * peers], log_src) * (1.0 / SCALE)
+    rows = row_out.shape[0]
+    own = pl.ds(pl.multiple_of(index[0] * rows, rows), rows)
+    row_out[...] = dual[own, :] * (1.0 / SCALE) + xn[own, :]
 
 
 def params(mib):
     return pltpu.CompilerParams(vmem_limit_bytes=mib * 2**20)
 
 
-def lse_pass(log_count, parts, prev, main, tail, rhs, copies):
+def lse_pass(log_count, parts, prev, main, tail, rhs, copies, norm=None):
     length, width = main.shape[0], rhs.shape[1]
+    norms = [] if norm is None else [norm]
+
+    def kernel(parts, prev, *refs):
+        at = len(norms)
+        pass_kernel(log_count, parts, prev, refs[0] if at else None, *refs[at:])
+
     return pl.pallas_call(
-        lambda *refs: pass_kernel(log_count, *refs),
+        kernel,
         out_shape=(
             jax.ShapeDtypeStruct((copies, width // LANES, LANES), f32),
             jax.ShapeDtypeStruct((length // LANES, LANES), f32),
         ),
-        in_specs=[vmem] * 5,
+        in_specs=[vmem] * (5 + len(norms)),
         out_specs=(vmem, vmem),
         scratch_shapes=[
             pltpu.VMEM((length, LANES), bf16),
             pltpu.VMEM((EDGE, width), bf16),
             pltpu.VMEM((length, WIDTH), f32),
         ],
-        compiler_params=params(20),
-    )(parts, prev, main, tail, rhs)
+        compiler_params=params(12),
+    )(parts, prev, *norms, main, tail, rhs)
 
 
 def gathered(value, axes):
@@ -199,10 +210,12 @@
 COL_GATHER = ("z", "yl")
 ROW_PEERS = ("yh", "core", "x")
 COL_PEERS = ("z", "yl")
+DEV = ("x", "z", "yl")
 
 
 def on_device(x_feat, y_feat):
     ring = lax.axis_size(ROW_GATHER)
+    index = lax.axis_index(ROW_GATHER).reshape(1)
     blocks = [x_feat]
     for shift in range(1, ring):
         pairs = [(i, (i + shift) % ring) for i in range(ring)]
@@ -229,36 +242,36 @@
             jax.ShapeDtypeStruct((1, cols // LANES, LANES), f32),
             jax.ShapeDtypeStruct((rows // LANES, LANES), f32),
         ],
-        in_specs=[pl.BlockSpec(memory_space=pltpu.SMEM)] + [vmem] * (ring + 1),
+        in_specs=[smem] + [vmem] * (ring + 1),
         out_specs=[vmem] * 10,
         compiler_params=params(20),
-    )(lax.axis_index(ROW_GATHER).reshape(1), *blocks, yg)
+    )(index, *blocks, yg)
     dual_x = before
     for iteration in range(ITERS):
         sums, dual_y = lse_pass(log_src, parts, dual_x, ym, yt, xr, row_peers)
         parts = exchanged(sums, ROW_PEERS)
-        sums, dual_x = lse_pass(log_tgt, parts, dual_y, xm, xt, yr, col_peers)
-        parts = exchanged(sums, COL_PEERS)
+        if iteration < ITERS - 1:
+            sums, dual_x = lse_pass(log_tgt, parts, dual_y, xm, xt, yr, col_peers)
+            parts = exchanged(sums, COL_PEERS)
+    sums, dual_x = lse_pass(log_tgt, parts, dual_y, xm, xt, yr, lax.axis_size(DEV), yn)
+    parts = exchanged(sums, DEV)
     dual_col, dual_row = pl.pallas_call(
         lambda *refs: final_kernel(log_src, *refs),
         out_shape=(
             jax.ShapeDtypeStruct((ring, cols // LANES, LANES), f32),
-            jax.ShapeDtypeStruct((rows // LANES, LANES), f32),
+            jax.ShapeDtypeStruct((x_feat.shape[1] // LANES, LANES), f32),
         ),
-        in_specs=[vmem] * 4,
+        in_specs=[smem] + [vmem] * 3,
         out_specs=(vmem, vmem),
-    )(parts, yn, dual_x, xn)
-    own = x_feat.shape[1] // LANES
-    dual_row = lax.dynamic_slice_in_dim(dual_row, lax.axis_index(ROW_GATHER) * own, own, 0)
-    dual_col = exchanged(dual_col, ROW_GATHER)
+        compiler_params=params(4),
+    )(index, parts, dual_x, xn)
     return dual_row.reshape(-1), dual_col.reshape(-1)
 
 
 def solution(mesh):
     fine = Mesh(mesh.devices.reshape(2, 2, 4, 4, 2), ("yh", "core", "x", "z", "yl"))
-    dev = ("x", "z", "yl")
-    in_specs = (P(None, dev), P(None, ("yh", "core") + dev))
-    out_specs = (P(dev), P(("yh", "core")))
+    in_specs = (P(None, DEV), P(None, ("yh", "core") + DEV))
+    out_specs = (P(DEV), P(("yh", "core")))
     return jax.shard_map(
         on_device, mesh=fine, in_specs=in_specs, out_specs=out_specs, check_vma=False
     )

time: 213 us -> 208 us (0.977)
  the two profiles are of different devices: /device:TPU:16 before, /device:TPU:1 now
where the time goes in v4:
time: 208 us; the launch traced here: 207 us
  Pallas kernels  109 us (52%)
  blocking collectives  72.9 us (35%)
  starting transfers between devices  12.4 us (6%)
  waiting for transfers between devices  9.93 us (5%)
    pallas_call x4, Pallas kernels, lse_pass(): pl.pallas_call(kernel, out_shape=(jax.ShapeDtypeStruct((copies, width //...  107 us
    all_to_all x4, blocking collectives, exchanged(): return lax.all_to_all(parts, axes, 0, 0, tiled=True)  72.9 us
    ppermute x3, waiting for transfers between devices, on_device(): blocks.append(lax.ppermute(x_feat, ROW_GATHER, pairs))  9.93 us
    all_to_all x1, starting transfers between devices, gathered(): return lax.all_to_all(copies, axes, 0, 0, tiled=True)  6.88 us
    ppermute x3, starting transfers between devices, on_device(): blocks.append(lax.ppermute(x_feat, ROW_GATHER, pairs))  5.5 us
  transfers between devices with their start and end apart: 4, of which 2 were waited for; matrix products, arithmetic and copies ran while one was open for 0% of the time, Pallas kernels for 0%

profile of v4, /device:TPU:1, one launch (start us, length us, event | category | flops | bytes accessed | tf_op | source)
XLA Modules:
  0.0 206.9 jit_solution(13535315651273596491)
XLA Ops:
  0.6 0.0 copy-start
  0.6 2.0 broadcast_in_dim.2
  2.7 6.9 %all-to-all-start = ((f32[8,64,512]{2,1,0:T(8,128)}), f32[8,64,512]{2,1,0:T(8,128)S(1)}, u32[]{:S(2)}, u32[]{:S(2)}) async-start(f32[8,64,512]{2,1,0:T(8,128)} %broadcast_in_dim.2), calls=%async_computation | async-start | bytes 2097152 | tf_op jit(solution)/shard_map/all_to_all | solution.py:202
  9.6 0.0 copy-done
  9.6 2.8 %collective-permute-start.1 = (f32[64,1024]{1,0:T(8,128)S(1)}, f32[64,1024]{1,0:T(8,128)S(1)}, u32[]{:S(2)}, u32[]{:S(2)}) collective-permute-start(f32[64,1024]{1,0:T(8,128)S(1)} %copy-done), channel_id=1, source_target_pairs={{0,16},{8,24},{16,0},{24,8},{1,17},{9,25},{17,1},{25,9},{2,18},{10... | collective-permute-start | bytes 786440 | tf_op jit(solution)/shard_map/ppermute | solution.py:222
  12.4 0.3 collective-permute-start
  12.7 2.4 %collective-permute-start.2 = (f32[64,1024]{1,0:T(8,128)S(1)}, f32[64,1024]{1,0:T(8,128)S(1)}, u32[]{:S(2)}, u32[]{:S(2)}) collective-permute-start(f32[64,1024]{1,0:T(8,128)S(1)} %copy-done), channel_id=1, source_target_pairs={{0,24},{8,0},{16,8},{24,16},{1,25},{9,1},{17,9},{25,17},{2,26},{10... | collective-permute-start | bytes 786440 | tf_op jit(solution)/shard_map/ppermute | solution.py:222
  15.1 3.0 %collective-permute-done.1.refs_3_ = f32[64,1024]{1,0:T(8,128)S(1)} collective-permute-done((f32[64,1024]{1,0:T(8,128)S(1)}, f32[64,1024]{1,0:T(8,128)S(1)}, u32[]{:S(2)}, u32[]{:S(2)}) %collective-permute-start.1) | collective-permute-done | bytes 262176 | tf_op jit(solution)/shard_map/ppermute | solution.py:222
  18.0 7.0 %collective-permute-done.refs_2_ = f32[64,1024]{1,0:T(8,128)S(1)} collective-permute-done((f32[64,1024]{1,0:T(8,128)S(1)}, f32[64,1024]{1,0:T(8,128)S(1)}, u32[]{:S(2)}, u32[]{:S(2)}) %collective-permute-start) | collective-permute-done | bytes 262176 | tf_op jit(solution)/shard_map/ppermute | solution.py:222
  25.0 0.0 collective-permute-done.2.refs_4_
  25.0 0.0 all-to-all-done.refs_5_
  25.0 1.2 shard_map.41
  26.3 32.0 %shard_map.42 = (f32[16,32,128]{2,1,0:T(8,128)S(1)}, f32[32,128]{1,0:T(8,128)S(1)}) custom-call(f32[1,32,128]{2,1,0:T(8,128)S(1)} %get-tuple-element.22.parts, f32[32,128]{1,0:T(8,128)S(1)} %get-tuple-element.23.prev, bf16[4096,128]{1,0:T(8,128)(2,1)S(1)} %get-tuple-element.24.refs_0_, bf16[4096,128]{1,0:T(8,128)(2,1)S(1)} %get-tuple-element.25.refs_1_, ...), custom_call_target="tpu_custom_call" | custom-call | tf_op jit(solution)/shard_map/pallas_call | solution.py:183
  58.2 16.4 %all_to_all.25.parts = f32[16,32,128]{2,1,0:T(8,128)S(1)} all-to-all(f32[16,32,128]{2,1,0:T(8,128)S(1)} %get-tuple-element.27), channel_id=1, replica_groups=mesh['yh'=2,'core'=2,'x'=4,'z'=4,'yl'=2] {'yh','core','x'}, dimensions={0} | all-to-all | bytes 524288 | tf_op jit(solution)/shard_map/all_to_all | solution.py:206
  74.6 31.8 %shard_map.43 = (f32[8,32,128]{2,1,0:T(8,128)S(1)}, f32[32,128]{1,0:T(8,128)S(1)}) custom-call(f32[16,32,128]{2,1,0:T(8,128)S(1)} %all_to_all.25.parts, f32[32,128]{1,0:T(8,128)S(1)} %get-tuple-element.28.prev, bf16[4096,128]{1,0:T(8,128)(2,1)S(1)} %get-tuple-element.29.refs_0_.refs_1_, bf16[4096,128]{1,0:T(8,128)(2,1)S(1)} %get-tuple-element.30.refs_1_.refs_2_, ...), custom_call_target="tpu_custom_call" | custom-call | tf_op jit(solution)/shard_map/pallas_call | solution.py:183
  106.4 8.8 %all_to_all.26.parts = f32[8,32,128]{2,1,0:T(8,128)S(1)} all-to-all(f32[8,32,128]{2,1,0:T(8,128)S(1)} %get-tuple-element.32), channel_id=1, replica_groups=mesh['yh'=2,'core'=2,'x'=4,'z'=4,'yl'=2] {'z','yl'}, dimensions={0} | all-to-all | bytes 262144 | tf_op jit(solution)/shard_map/all_to_all | solution.py:206
  115.3 32.0 %shard_map.44 = (f32[16,32,128]{2,1,0:T(8,128)S(1)}, f32[32,128]{1,0:T(8,128)S(1)}) custom-call(f32[8,32,128]{2,1,0:T(8,128)S(1)} %all_to_all.26.parts, f32[32,128]{1,0:T(8,128)S(1)} %get-tuple-element.33.prev, bf16[4096,128]{1,0:T(8,128)(2,1)S(1)} %get-tuple-element.24.refs_0_, bf16[4096,128]{1,0:T(8,128)(2,1)S(1)} %get-tuple-element.25.refs_1_, ...), custom_call_target="tpu_custom_call" | custom-call | tf_op jit(solution)/shard_map/pallas_call | solution.py:183
  147.2 14.2 %all_to_all.27.parts = f32[16,32,128]{2,1,0:T(8,128)S(1)} all-to-all(f32[16,32,128]{2,1,0:T(8,128)S(1)} %get-tuple-element.34), channel_id=1, replica_groups=mesh['yh'=2,'core'=2,'x'=4,'z'=4,'yl'=2] {'yh','core','x'}, dimensions={0} | all-to-all | bytes 524288 | tf_op jit(solution)/shard_map/all_to_all | solution.py:206
  161.4 11.2 %shard_map.45 = (f32[32,32,128]{2,1,0:T(8,128)S(1)}, f32[32,128]{1,0:T(8,128)S(1)}) custom-call(f32[16,32,128]{2,1,0:T(8,128)S(1)} %all_to_all.27.parts, f32[32,128]{1,0:T(8,128)S(1)} %get-tuple-element.35.prev, f32[32,128]{1,0:T(8,128)S(1)} %get-tuple-element.36.refs_0_, bf16[4096,128]{1,0:T(8,128)(2,1)S(1)} %get-tuple-element.29.refs_0_.refs_1_, ...), custom_call_target="tpu_custom_call" | custom-call | tf_op jit(solution)/shard_map/pallas_call | solution.py:183
  172.7 33.5 %all_to_all.28.refs_1_ = f32[32,32,128]{2,1,0:T(8,128)S(1)} all-to-all(f32[32,32,128]{2,1,0:T(8,128)S(1)} %get-tuple-element.37), channel_id=1, replica_groups=mesh['yh'=2,'core'=2,'x'=4,'z'=4,'yl'=2] {'x','z','yl'}, dimensions={0} | all-to-all | bytes 1048576 | tf_op jit(solution)/shard_map/all_to_all | solution.py:206
  206.1 0.7 shard_map.46
Async XLA Ops:
  0.6 8.9 %copy-start = (f32[64,1024]{1,0:T(8,128)S(1)}, f32[64,1024]{1,0:T(8,128)}, u32[]{:S(2)}) copy-start(f32[64,1024]{1,0:T(8,128)} %refs_1_.1) | copy-start | bytes 786436
  2.7 22.3 %all-to-all-start = ((f32[8,64,512]{2,1,0:T(8,128)}), f32[8,64,512]{2,1,0:T(8,128)S(1)}, u32[]{:S(2)}, u32[]{:S(2)}) async-start(f32[8,64,512]{2,1,0:T(8,128)} %broadcast_in_dim.2), calls=%async_computation | async-start | bytes 2097152 | tf_op jit(solution)/shard_map/all_to_all | solution.py:202
  9.6 8.5 %collective-permute-start.1 = (f32[64,1024]{1,0:T(8,128)S(1)}, f32[64,1024]{1,0:T(8,128)S(1)}, u32[]{:S(2)}, u32[]{:S(2)}) collective-permute-start(f32[64,1024]{1,0:T(8,128)S(1)} %copy-done), channel_id=1, source_target_pairs={{0,16},{8,24},{16,0},{24,8},{1,17},{9,25},{17,1},{25,9},{2,18},{10... | collective-permute-start | bytes 786440 | tf_op jit(solution)/shard_map/ppermute | solution.py:222
  12.4 12.6 %collective-permute-start = (f32[64,1024]{1,0:T(8,128)S(1)}, f32[64,1024]{1,0:T(8,128)S(1)}, u32[]{:S(2)}, u32[]{:S(2)}) collective-permute-start(f32[64,1024]{1,0:T(8,128)S(1)} %copy-done), channel_id=1, source_target_pairs={{0,8},{8,16},{16,24},{24,0},{1,9},{9,17},{17,25},{25,1},{2,10},{10... | collective-permute-start | bytes 786440 | tf_op jit(solution)/shard_map/ppermute | solution.py:222
  12.7 12.3 %collective-permute-start.2 = (f32[64,1024]{1,0:T(8,128)S(1)}, f32[64,1024]{1,0:T(8,128)S(1)}, u32[]{:S(2)}, u32[]{:S(2)}) collective-permute-start(f32[64,1024]{1,0:T(8,128)S(1)} %copy-done), channel_id=1, source_target_pairs={{0,24},{8,0},{16,8},{24,16},{1,25},{9,1},{17,9},{25,17},{2,26},{10... | collective-permute-start | bytes 786440 | tf_op jit(solution)/shard_map/ppermute | solution.py:222

commit v5 on v4

--- a/solution.py
+++ b/solution.py
@@ -193,12 +193,23 @@
             pltpu.VMEM((EDGE, width), bf16),
             pltpu.VMEM((length, WIDTH), f32),
         ],
-        compiler_params=params(12),
+        compiler_params=params(9),
     )(parts, prev, *norms, main, tail, rhs)
 
 
+def repeat_kernel(value, out):
+    for i in range(out.shape[0]):
+        out[i] = value[...]
+
+
 def gathered(value, axes):
-    copies = jnp.broadcast_to(value[None], (lax.axis_size(axes),) + value.shape)
+    copies = pl.pallas_call(
+        repeat_kernel,
+        out_shape=jax.ShapeDtypeStruct((lax.axis_size(axes),) + value.shape, value.dtype),
+        in_specs=[vmem],
+        out_specs=vmem,
+        compiler_params=params(4),
+    )(value)
     return lax.all_to_all(copies, axes, 0, 0, tiled=True)
 
 
@@ -244,7 +255,7 @@
         ],
         in_specs=[smem] + [vmem] * (ring + 1),
         out_specs=[vmem] * 10,
-        compiler_params=params(20),
+        compiler_params=params(9),
     )(index, *blocks, yg)
     dual_x = before
     for iteration in range(ITERS):

time: 208 us -> 207 us (level)
  no operation moved by 1% of the time
where the time goes in v5:
time: 207 us; the launch traced here: 206 us
  Pallas kernels  109 us (53%)
  blocking collectives  73.4 us (35%)
  starting transfers between devices  12.4 us (6%)
  waiting for transfers between devices  9.93 us (5%)
    pallas_call x4, Pallas kernels, lse_pass(): pl.pallas_call(kernel, out_shape=(jax.ShapeDtypeStruct((copies, width //...  106 us
    all_to_all x4, blocking collectives, exchanged(): return lax.all_to_all(parts, axes, 0, 0, tiled=True)  73.4 us
    ppermute x3, waiting for transfers between devices, on_device(): blocks.append(lax.ppermute(x_feat, ROW_GATHER, pairs))  9.93 us
    all_to_all x1, starting transfers between devices, gathered(): return lax.all_to_all(copies, axes, 0, 0, tiled=True)  6.88 us
    ppermute x3, starting transfers between devices, on_device(): blocks.append(lax.ppermute(x_feat, ROW_GATHER, pairs))  5.5 us
  transfers between devices with their start and end apart: 4, of which 2 were waited for; matrix products, arithmetic and copies ran while one was open for 0% of the time, Pallas kernels for 0%

profile of v5, /device:TPU:1, one launch (start us, length us, event | category | flops | bytes accessed | tf_op | source)
XLA Modules:
  0.0 206.3 jit_solution(3867322233802001563)
XLA Ops:
  0.6 0.0 copy-start.1
  0.6 0.9 copy-done.1
  1.5 0.0 copy-start
  1.5 1.0 shard_map.41
  2.6 6.9 %all-to-all-start = ((f32[8,64,512]{2,1,0:T(8,128)}), f32[8,64,512]{2,1,0:T(8,128)S(1)}, u32[]{:S(2)}, u32[]{:S(2)}) async-start(f32[8,64,512]{2,1,0:T(8,128)} %shard_map.41), calls=%async_computation | async-start | bytes 2097152 | tf_op jit(solution)/shard_map/all_to_all | solution.py:213
  9.5 0.0 copy-done
  9.5 2.8 %collective-permute-start.1 = (f32[64,1024]{1,0:T(8,128)S(1)}, f32[64,1024]{1,0:T(8,128)S(1)}, u32[]{:S(2)}, u32[]{:S(2)}) collective-permute-start(f32[64,1024]{1,0:T(8,128)S(1)} %copy-done), channel_id=1, source_target_pairs={{0,16},{8,24},{16,0},{24,8},{1,17},{9,25},{17,1},{25,9},{2,18},{10... | collective-permute-start | bytes 786440 | tf_op jit(solution)/shard_map/ppermute | solution.py:233
  12.3 0.3 collective-permute-start
  12.6 2.4 %collective-permute-start.2 = (f32[64,1024]{1,0:T(8,128)S(1)}, f32[64,1024]{1,0:T(8,128)S(1)}, u32[]{:S(2)}, u32[]{:S(2)}) collective-permute-start(f32[64,1024]{1,0:T(8,128)S(1)} %copy-done), channel_id=1, source_target_pairs={{0,24},{8,0},{16,8},{24,16},{1,25},{9,1},{17,9},{25,17},{2,26},{10... | collective-permute-start | bytes 786440 | tf_op jit(solution)/shard_map/ppermute | solution.py:233
  15.0 3.0 %collective-permute-done.1.refs_3_ = f32[64,1024]{1,0:T(8,128)S(1)} collective-permute-done((f32[64,1024]{1,0:T(8,128)S(1)}, f32[64,1024]{1,0:T(8,128)S(1)}, u32[]{:S(2)}, u32[]{:S(2)}) %collective-permute-start.1) | collective-permute-done | bytes 262176 | tf_op jit(solution)/shard_map/ppermute | solution.py:233
  17.9 7.0 %collective-permute-done.refs_2_ = f32[64,1024]{1,0:T(8,128)S(1)} collective-permute-done((f32[64,1024]{1,0:T(8,128)S(1)}, f32[64,1024]{1,0:T(8,128)S(1)}, u32[]{:S(2)}, u32[]{:S(2)}) %collective-permute-start) | collective-permute-done | bytes 262176 | tf_op jit(solution)/shard_map/ppermute | solution.py:233
  24.9 0.0 collective-permute-done.2.refs_4_
  24.9 0.0 all-to-all-done.refs_5_
  24.9 1.2 shard_map.42
  26.2 31.9 %shard_map.43 = (f32[16,32,128]{2,1,0:T(8,128)S(1)}, f32[32,128]{1,0:T(8,128)S(1)}) custom-call(f32[1,32,128]{2,1,0:T(8,128)S(1)} %get-tuple-element.22.parts, f32[32,128]{1,0:T(8,128)S(1)} %get-tuple-element.23.prev, bf16[4096,128]{1,0:T(8,128)(2,1)S(1)} %get-tuple-element.24.refs_0_, bf16[4096,128]{1,0:T(8,128)(2,1)S(1)} %get-tuple-element.25.refs_1_, ...), custom_call_target="tpu_custom_call" | custom-call | tf_op jit(solution)/shard_map/pallas_call | solution.py:183
  58.1 16.4 %all_to_all.25.parts = f32[16,32,128]{2,1,0:T(8,128)S(1)} all-to-all(f32[16,32,128]{2,1,0:T(8,128)S(1)} %get-tuple-element.27), channel_id=1, replica_groups=mesh['yh'=2,'core'=2,'x'=4,'z'=4,'yl'=2] {'yh','core','x'}, dimensions={0} | all-to-all | bytes 524288 | tf_op jit(solution)/shard_map/all_to_all | solution.py:217
  74.5 31.3 %shard_map.44 = (f32[8,32,128]{2,1,0:T(8,128)S(1)}, f32[32,128]{1,0:T(8,128)S(1)}) custom-call(f32[16,32,128]{2,1,0:T(8,128)S(1)} %all_to_all.25.parts, f32[32,128]{1,0:T(8,128)S(1)} %get-tuple-element.28.prev, bf16[4096,128]{1,0:T(8,128)(2,1)S(1)} %get-tuple-element.29.refs_0_.refs_1_, bf16[4096,128]{1,0:T(8,128)(2,1)S(1)} %get-tuple-element.30.refs_1_.refs_2_, ...), custom_call_target="tpu_custom_call" | custom-call | tf_op jit(solution)/shard_map/pallas_call | solution.py:183
  105.8 8.8 %all_to_all.26.parts = f32[8,32,128]{2,1,0:T(8,128)S(1)} all-to-all(f32[8,32,128]{2,1,0:T(8,128)S(1)} %get-tuple-element.32), channel_id=1, replica_groups=mesh['yh'=2,'core'=2,'x'=4,'z'=4,'yl'=2] {'z','yl'}, dimensions={0} | all-to-all | bytes 262144 | tf_op jit(solution)/shard_map/all_to_all | solution.py:217
  114.6 31.9 %shard_map.45 = (f32[16,32,128]{2,1,0:T(8,128)S(1)}, f32[32,128]{1,0:T(8,128)S(1)}) custom-call(f32[8,32,128]{2,1,0:T(8,128)S(1)} %all_to_all.26.parts, f32[32,128]{1,0:T(8,128)S(1)} %get-tuple-element.33.prev, bf16[4096,128]{1,0:T(8,128)(2,1)S(1)} %get-tuple-element.24.refs_0_, bf16[4096,128]{1,0:T(8,128)(2,1)S(1)} %get-tuple-element.25.refs_1_, ...), custom_call_target="tpu_custom_call" | custom-call | tf_op jit(solution)/shard_map/pallas_call | solution.py:183
  146.6 14.2 %all_to_all.27.parts = f32[16,32,128]{2,1,0:T(8,128)S(1)} all-to-all(f32[16,32,128]{2,1,0:T(8,128)S(1)} %get-tuple-element.34), channel_id=1, replica_groups=mesh['yh'=2,'core'=2,'x'=4,'z'=4,'yl'=2] {'yh','core','x'}, dimensions={0} | all-to-all | bytes 524288 | tf_op jit(solution)/shard_map/all_to_all | solution.py:217
  160.8 10.9 %shard_map.46 = (f32[32,32,128]{2,1,0:T(8,128)S(1)}, f32[32,128]{1,0:T(8,128)S(1)}) custom-call(f32[16,32,128]{2,1,0:T(8,128)S(1)} %all_to_all.27.parts, f32[32,128]{1,0:T(8,128)S(1)} %get-tuple-element.35.prev, f32[32,128]{1,0:T(8,128)S(1)} %get-tuple-element.36.refs_0_, bf16[4096,128]{1,0:T(8,128)(2,1)S(1)} %get-tuple-element.29.refs_0_.refs_1_, ...), custom_call_target="tpu_custom_call" | custom-call | tf_op jit(solution)/shard_map/pallas_call | solution.py:183
  171.7 33.9 %all_to_all.28.refs_1_ = f32[32,32,128]{2,1,0:T(8,128)S(1)} all-to-all(f32[32,32,128]{2,1,0:T(8,128)S(1)} %get-tuple-element.37), channel_id=1, replica_groups=mesh['yh'=2,'core'=2,'x'=4,'z'=4,'yl'=2] {'x','z','yl'}, dimensions={0} | all-to-all | bytes 1048576 | tf_op jit(solution)/shard_map/all_to_all | solution.py:217
  205.6 0.7 shard_map.47
Async XLA Ops:
  0.6 0.9 copy-start.1
  1.5 7.9 %copy-start = (f32[64,1024]{1,0:T(8,128)S(1)}, f32[64,1024]{1,0:T(8,128)}, u32[]{:S(2)}) copy-start(f32[64,1024]{1,0:T(8,128)} %refs_1_.1) | copy-start | bytes 786436
  2.6 22.3 %all-to-all-start = ((f32[8,64,512]{2,1,0:T(8,128)}), f32[8,64,512]{2,1,0:T(8,128)S(1)}, u32[]{:S(2)}, u32[]{:S(2)}) async-start(f32[8,64,512]{2,1,0:T(8,128)} %shard_map.41), calls=%async_computation | async-start | bytes 2097152 | tf_op jit(solution)/shard_map/all_to_all | solution.py:213
  9.5 8.5 %collective-permute-start.1 = (f32[64,1024]{1,0:T(8,128)S(1)}, f32[64,1024]{1,0:T(8,128)S(1)}, u32[]{:S(2)}, u32[]{:S(2)}) collective-permute-start(f32[64,1024]{1,0:T(8,128)S(1)} %copy-done), channel_id=1, source_target_pairs={{0,16},{8,24},{16,0},{24,8},{1,17},{9,25},{17,1},{25,9},{2,18},{10... | collective-permute-start | bytes 786440 | tf_op jit(solution)/shard_map/ppermute | solution.py:233
  12.3 12.6 %collective-permute-start = (f32[64,1024]{1,0:T(8,128)S(1)}, f32[64,1024]{1,0:T(8,128)S(1)}, u32[]{:S(2)}, u32[]{:S(2)}) collective-permute-start(f32[64,1024]{1,0:T(8,128)S(1)} %copy-done), channel_id=1, source_target_pairs={{0,8},{8,16},{16,24},{24,0},{1,9},{9,17},{17,25},{25,1},{2,10},{10... | collective-permute-start | bytes 786440 | tf_op jit(solution)/shard_map/ppermute | solution.py:233
  12.6 12.3 %collective-permute-start.2 = (f32[64,1024]{1,0:T(8,128)S(1)}, f32[64,1024]{1,0:T(8,128)S(1)}, u32[]{:S(2)}, u32[]{:S(2)}) collective-permute-start(f32[64,1024]{1,0:T(8,128)S(1)} %copy-done), channel_id=1, source_target_pairs={{0,24},{8,0},{16,8},{24,16},{1,25},{9,1},{17,9},{25,17},{2,26},{10... | collective-permute-start | bytes 786440 | tf_op jit(solution)/shard_map/ppermute | solution.py:233

commit v6 on v5

--- a/solution.py
+++ b/solution.py
@@ -20,6 +20,7 @@
 ACC_ROWS = 16
 DUAL_LANE = 64
 EDGE = 64
+SUBLANES = 8
 SMALLEST = 2.0**-80
 
 f32 = jnp.float32
@@ -55,17 +56,6 @@
     tail[here, :] = jnp.transpose(jnp.concatenate([low, jnp.zeros_like(low)], axis=0))
 
 
-def prepare_kernel(log_src, index, *refs):
-    xs, (y_ref, xm, xt, xr, xn, ym, yt, yr, yn, first, before) = refs[:-11], refs[-11:]
-    for shift, x_ref in enumerate(xs):
-        at = lax.rem(index[0] + len(xs) - shift, len(xs))
-        prepare_block(x_ref[...], at, xm, xt, xr, xn, 2.0 * SCALE)
-    for at in range(y_ref.shape[0]):
-        prepare_block(y_ref[at], at, ym, yt, yr, yn, 1.0)
-    first[0] = log_src + SCALE * yn[...]
-    before[...] = log_src - SCALE * xn[...]
-
-
 def combine(parts, log_count):
     peak = parts[0]
     for i in range(1, parts.shape[0]):
@@ -82,80 +72,147 @@
     return high, mid, value - high - mid
 
 
-def placed(parts, row, height, first):
-    place = lax.broadcasted_iota(jnp.int32, (height, LANES), 0)
-    value = jnp.zeros((height, LANES), f32)
+def stacked(parts, row, ones):
+    place = lax.broadcasted_iota(jnp.int32, (SUBLANES, LANES), 0)
+    value = jnp.where(place < 6, 1.0, 0.0)
     for i, part in enumerate(parts):
-        value = jnp.where(place == first + i, part[row : row + 1], value)
+        value = jnp.where(place == (3 - ones) + i, part[row : row + 1], value)
     return value
 
 
-def pass_kernel(log_count, parts, prev, norm, main, tail, rhs, out, dual_out, full, edge, score):
-    length, width = main.shape[0], rhs.shape[1]
+def fill_duals(dual, tail, full):
+    parts = split3(dual)
+    before = jnp.zeros((DUAL_LANE, LANES), f32)
+    after = jnp.zeros((LANES - DUAL_LANE - SUBLANES, LANES), f32)
+    for k in range(dual.shape[0]):
+        here = pl.ds(k * LANES, LANES)
+        rows = jnp.concatenate([before, stacked(parts, k, 3), after], axis=0)
+        full[here, :] = (tail[here, :].astype(f32) + jnp.transpose(rows)).astype(bf16)
+
+
+def fill_bounds(bound, edge, start):
+    parts = split3(-bound)
+    cells = bound.shape[0] * LANES
+    edge[2 * SUBLANES :, pl.ds(start, cells)] = jnp.zeros((EDGE - 2 * SUBLANES, cells), bf16)
+    for k in range(bound.shape[0]):
+        rows = jnp.concatenate([stacked(parts, k, 0), jnp.zeros((SUBLANES, LANES), f32)], axis=0)
+        edge[0 : 2 * SUBLANES, pl.ds(start + k * LANES, LANES)] = rows.astype(bf16)
+
+
+def column_logs(main, full, rhs, edge, logs, partial, low, count):
+    chunks = main.shape[0] // CHUNK
+    rows_of = WIDTH // LANES
+
+    def scores(block, chunk):
+        here = pl.ds(chunk * CHUNK, CHUNK)
+        if not isinstance(chunk, int):
+            here = pl.ds(pl.multiple_of(chunk * CHUNK, CHUNK), CHUNK)
+        cols = pl.ds(pl.multiple_of(block * WIDTH, WIDTH), WIDTH)
+        lhs = jnp.concatenate([main[here, :], full[here, :]], axis=1)
+        weight = jnp.concatenate([rhs[:, cols], edge[:, cols]], axis=0)
+        return jnp.dot(lhs, weight, preferred_element_type=f32)
+
+    def finish(block, value):
+        for q in range(rows_of):
+            logs[pl.ds(block * rows_of + q, 1), :] = value[:, q * LANES : (q + 1) * LANES]
+
+    zero = jnp.zeros((ACC_ROWS, WIDTH), f32)
+
+    def step(group, carry):
+        for t in range(GROUP):
+            block, acc = group * GROUP + t, zero
+            for chunk in range(chunks):
+                acc = fold(jnp.add, acc, jnp.exp2(scores(low + block, chunk)))
+            here = pl.ds(pl.multiple_of(block * SUBLANES, SUBLANES), SUBLANES)
+            partial[here, :] = fold(jnp.add, acc[:SUBLANES], acc[SUBLANES:])
+        return carry
+
+    lax.fori_loop(0, count // GROUP, step, 0)
+    least = jnp.full((1, WIDTH), 1.0, f32)
+    for block in range(count):
+        total = jnp.sum(partial[block * SUBLANES : (block + 1) * SUBLANES, :], axis=0, keepdims=True)
+        least = jnp.minimum(least, total)
+        finish(low + block, jnp.log2(total))
+
+    @pl.when(jnp.min(least) < SMALLEST)
+    def _():
+        def exact(block, carry):
+            def peaks(chunk, peak):
+                return fold(jnp.maximum, peak, scores(low + block, chunk))
+
+            peak = lax.fori_loop(0, chunks, peaks, jnp.full((ACC_ROWS, WIDTH), -jnp.inf, f32))
+            top = jnp.max(peak, axis=0, keepdims=True)
+
+            def sums(chunk, acc):
+                return fold(jnp.add, acc, jnp.exp2(scores(low + block, chunk) - top))
+
+            acc = lax.fori_loop(0, chunks, sums, zero)
+            finish(low + block, top + jnp.log2(jnp.sum(acc, axis=0, keepdims=True)))
+            return carry
+
+        lax.fori_loop(0, count, exact, 0)
+
+
+def pass_kernel(log_count, parts, prev, norm, main, tail, rhs, out, dual_out, full, edge, logs, partial):
     dual = combine(parts, log_count)
     dual_out[...] = dual
     bound = log_count - prev[...]
-    duals, bounds = split3(dual), split3(-bound)
-    place = lax.broadcasted_iota(jnp.int32, (LANES, LANES), 0)
-    for k in range(length // LANES):
-        here = pl.ds(k * LANES, LANES)
-        rows = placed(duals, k, LANES, DUAL_LANE)
-        rows = jnp.where((place >= DUAL_LANE + 3) & (place < DUAL_LANE + 6), 1.0, rows)
-        full[here, :] = (tail[here, :].astype(f32) + jnp.transpose(rows)).astype(bf16)
-    place = lax.broadcasted_iota(jnp.int32, (EDGE, LANES), 0)
-    for k in range(width // LANES):
-        rows = jnp.where(place < 3, 1.0, placed(bounds, k, EDGE, 3))
-        edge[:, pl.ds(k * LANES, LANES)] = rows.astype(bf16)
-
-    def scores(block, chunk):
-        here = pl.ds(chunk * CHUNK, CHUNK)
-        lhs = jnp.concatenate([main[here, :], full[here, :]], axis=1)
-        cols = pl.ds(pl.multiple_of(block * WIDTH, WIDTH), WIDTH)
-        weight = jnp.concatenate([rhs[:, cols], edge[:, cols]], axis=0)
-        return jnp.dot(lhs, weight, preferred_element_type=f32)
-
-    def finish(block, value):
-        for q in range(WIDTH // LANES):
-            row = block * (WIDTH // LANES) + q
-            piece = value[:, q * LANES : (q + 1) * LANES][None]
-            out[:, pl.ds(row, 1), :] = jnp.broadcast_to(piece, (out.shape[0], 1, LANES))
-
-    chunks, blocks = length // CHUNK, width // WIDTH
-    zero = jnp.zeros((ACC_ROWS, WIDTH), f32)
-
-    def step(group, least):
-        for t in range(GROUP):
-            block = group * GROUP + t
-            acc = zero
-            for chunk in range(chunks):
-                acc = fold(jnp.add, acc, jnp.exp2(scores(block, chunk)))
-            total = jnp.sum(acc, axis=0, keepdims=True)
-            least = jnp.minimum(least, total)
-            finish(block, jnp.log2(total))
-        return least
-
-    least = lax.fori_loop(0, blocks // GROUP, step, jnp.full((1, WIDTH), 1.0, f32))
-
-    @pl.when(jnp.min(least) < SMALLEST)
-    def _():
-        def exact(block, carry):
-            peak = jnp.full((ACC_ROWS, WIDTH), -jnp.inf, f32)
-            for chunk in range(chunks):
-                value = scores(block, chunk)
-                score[pl.ds(chunk * CHUNK, CHUNK), :] = value
-                peak = fold(jnp.maximum, peak, value)
-            top = jnp.max(peak, axis=0, keepdims=True)
-            acc = zero
-            for chunk in range(chunks):
-                acc = fold(jnp.add, acc, jnp.exp2(score[pl.ds(chunk * CHUNK, CHUNK), :] - top))
-            finish(block, top + jnp.log2(jnp.sum(acc, axis=0, keepdims=True)))
-            return carry
-
-        lax.fori_loop(0, blocks, exact, 0)
-
+    fill_duals(dual, tail, full)
+    fill_bounds(bound, edge, 0)
+    column_logs(main, full, rhs, edge, logs, partial, 0, rhs.shape[1] // WIDTH)
     offset = bound if norm is None else bound - SCALE * norm[...]
+    value = logs[...] + offset
     for i in range(out.shape[0]):
-        out[i] = out[i] + offset
+        out[i] = value
+
+
+def place_of(index, shift, ring):
+    return lax.rem(index[0] + (ring - shift), ring)
+
+
+def source_block(value, at, xm, xt, xr, xn, edge):
+    cells = value.shape[1]
+    prepare_block(value, at, xm, xt, xr, xn, 2.0 * SCALE)
+    rows = cells // LANES
+    here = pl.ds(pl.multiple_of(at * rows, rows), rows)
+    fill_bounds(SCALE * xn[here, :], edge, pl.multiple_of(at * cells, cells))
+
+
+def first_kernel(x_ref, y_ref, ym, yt, yr, yn, yf, dual_out, xm, xt, xr, xn, logs, edge, partial):
+    for at in range(y_ref.shape[0]):
+        prepare_block(y_ref[at], at, ym, yt, yr, yn, 1.0)
+    dual = -SCALE * yn[...]
+    dual_out[...] = dual
+    fill_duals(dual, yt, yf)
+    source_block(x_ref[...], 0, xm, xt, xr, xn, edge)
+    column_logs(ym, yf, xr, edge, logs, partial, 0, x_ref.shape[1] // WIDTH)
+
+
+def second_kernel(ring, index, *refs):
+    xs, refs = refs[: ring - 1], refs[ring - 1 :]
+    ym, yf, own_m, own_t, own_r, own_n, own_logs = refs[:7]
+    xm, xt, xr, xn, out, edge, logs, partial = refs[7:]
+    cells, rows = own_m.shape[0], own_n.shape[0]
+    at = place_of(index, 0, ring)
+    here = pl.ds(pl.multiple_of(at * cells, cells), cells)
+    xm[here, :] = own_m[...]
+    xt[here, :] = own_t[...]
+    xr[:, here] = own_r[...]
+    here = pl.ds(pl.multiple_of(at * rows, rows), rows)
+    xn[here, :] = own_n[...]
+    logs[here, :] = own_logs[...]
+    for shift, x_ref in enumerate(xs, 1):
+        source_block(x_ref[...], place_of(index, shift, ring), xm, xt, xr, xn, edge)
+    count = xs[0].shape[1] // WIDTH
+
+    def block(shift, carry):
+        column_logs(ym, yf, xr, edge, logs, partial, place_of(index, shift, ring) * count, count)
+        return carry
+
+    lax.fori_loop(1, ring, block, 0)
+    value = logs[...] + SCALE * xn[...]
+    for i in range(out.shape[0]):
+        out[i] = value
 
 
 def final_kernel(log_src, index, parts, dual, xn, col_out, row_out):
@@ -170,6 +227,11 @@
 
 def params(mib):
     return pltpu.CompilerParams(vmem_limit_bytes=mib * 2**20)
+
+
+def cost(rows, cols):
+    pairs = rows * cols
+    return pl.CostEstimate(flops=512 * pairs, bytes_accessed=pairs // 8, transcendentals=pairs)
 
 
 def lse_pass(log_count, parts, prev, main, tail, rhs, copies, norm=None):
@@ -191,7 +253,8 @@
         scratch_shapes=[
             pltpu.VMEM((length, LANES), bf16),
             pltpu.VMEM((EDGE, width), bf16),
-            pltpu.VMEM((length, WIDTH), f32),
+            pltpu.VMEM((width // LANES, LANES), f32),
+            pltpu.VMEM((width // WIDTH * SUBLANES, WIDTH), f32),
         ],
         compiler_params=params(9),
     )(parts, prev, *norms, main, tail, rhs)
@@ -245,25 +308,42 @@
             jax.ShapeDtypeStruct((cells // LANES, LANES), f32),
         ]
 
-    xm, xt, xr, xn, ym, yt, yr, yn, parts, before = pl.pallas_call(
-        lambda *refs: prepare_kernel(log_src, *refs),
-        out_shape=side(rows)
-        + side(cols)
-        + [
-            jax.ShapeDtypeStruct((1, cols // LANES, LANES), f32),
-            jax.ShapeDtypeStruct((rows // LANES, LANES), f32),
+    def dual_of(cells):
+        return jax.ShapeDtypeStruct((cells // LANES, LANES), f32)
+
+    block = x_feat.shape[1]
+    partial = pltpu.VMEM((block // WIDTH * SUBLANES, WIDTH), f32)
+    ym, yt, yr, yn, yf, dual_y, *own = pl.pallas_call(
+        first_kernel,
+        out_shape=side(cols)
+        + [jax.ShapeDtypeStruct((cols, LANES), bf16), dual_of(cols)]
+        + side(block)
+        + [dual_of(block)],
+        in_specs=[vmem] * 2,
+        out_specs=[vmem] * 11,
+        scratch_shapes=[pltpu.VMEM((EDGE, block), bf16), partial],
+        compiler_params=params(6),
+        cost_estimate=cost(block, cols),
+    )(x_feat, yg)
+    xm, xt, xr, xn, sums = pl.pallas_call(
+        lambda *refs: second_kernel(ring, *refs),
+        out_shape=side(rows) + [jax.ShapeDtypeStruct((row_peers, rows // LANES, LANES), f32)],
+        in_specs=[smem] + [vmem] * (ring + 6),
+        out_specs=[vmem] * 5,
+        scratch_shapes=[
+            pltpu.VMEM((EDGE, rows), bf16),
+            pltpu.VMEM((rows // LANES, LANES), f32),
+            partial,
         ],
-        in_specs=[smem] + [vmem] * (ring + 1),
-        out_specs=[vmem] * 10,
-        compiler_params=params(9),
-    )(index, *blocks, yg)
-    dual_x = before
-    for iteration in range(ITERS):
+        compiler_params=params(6),
+        cost_estimate=cost(rows - block, cols),
+    )(index, *blocks[1:], ym, yf, *own)
+    parts = exchanged(sums, ROW_PEERS)
+    for iteration in range(1, ITERS):
+        sums, dual_x = lse_pass(log_tgt, parts, dual_y, xm, xt, yr, col_peers)
+        parts = exchanged(sums, COL_PEERS)
         sums, dual_y = lse_pass(log_src, parts, dual_x, ym, yt, xr, row_peers)
         parts = exchanged(sums, ROW_PEERS)
-        if iteration < ITERS - 1:
-            sums, dual_x = lse_pass(log_tgt, parts, dual_y, xm, xt, yr, col_peers)
-            parts = exchanged(sums, COL_PEERS)
     sums, dual_x = lse_pass(log_tgt, parts, dual_y, xm, xt, yr, lax.axis_size(DEV), yn)
     parts = exchanged(sums, DEV)
     dual_col, dual_row = pl.pallas_call(

time: 207 us -> 440 us (2.13)
  Pallas kernels: 109 us -> 363 us
  blocking collectives: 73.4 us -> 52.9 us
    pallas_call x4 -> x3, Pallas kernels: 106 us -> 244 us  [lse_pass(): pl.pallas_call(kernel, out_shape=(jax.ShapeDtypeStruct((copies, width //...]
    pallas_call x1 -> x2, Pallas kernels: 1.25 us -> 118 us  [the longest x1 87.6 us: on_device(): pl.pallas_call(lambda *refs: second_kernel(ring, *refs), out_shape=side(r...]
    all_to_all x4, blocking collectives: 73.4 us -> 52.9 us  [exchanged(): return lax.all_to_all(parts, axes, 0, 0, tiled=True)]
    ppermute x3, waiting for transfers between devices: 9.93 us -> 0.01 us  [on_device(): blocks.append(lax.ppermute(x_feat, ROW_GATHER, pairs))]
    all_to_all x1, waiting for transfers between devices: 0.01 us -> 8.99 us  [gathered(): return lax.all_to_all(copies, axes, 0, 0, tiled=True)]
  transfers between devices with their start and end apart: 4 -> 4, of which waited for: 2 -> 1; matrix products, arithmetic and copies ran while one was open for 0% -> 0% of each run, Pallas kernels for 0% -> 7%
where the time goes in v6:
time: 440 us; the launch traced here: 439 us
  Pallas kernels  363 us (82%)
  blocking collectives  52.9 us (12%)
  starting transfers between devices  12.4 us (3%)
  waiting for transfers between devices  9 us (2%)
    pallas_call x3, Pallas kernels, lse_pass(): pl.pallas_call(kernel, out_shape=(jax.ShapeDtypeStruct((copies, width //...  244 us
    pallas_call x1, Pallas kernels, on_device(): pl.pallas_call(lambda *refs: second_kernel(ring, *refs), out_shape=side(r...  87.6 us
    all_to_all x4, blocking collectives, exchanged(): return lax.all_to_all(parts, axes, 0, 0, tiled=True)  52.9 us
    pallas_call x1, Pallas kernels, on_device(): pl.pallas_call(first_kernel, out_shape=side(cols) + [jax.ShapeDtypeStruct...  30.2 us
    all_to_all x1, waiting for transfers between devices, gathered(): return lax.all_to_all(copies, axes, 0, 0, tiled=True)  8.99 us
  transfers between devices with their start and end apart: 4, of which 1 were waited for; matrix products, arithmetic and copies ran while one was open for 0% of the time, Pallas kernels for 7%

profile of v6, /device:TPU:1, one launch (start us, length us, event | category | flops | bytes accessed | tf_op | source)
XLA Modules:
  0.0 439.3 jit_solution(686292524481791052)
XLA Ops:
  0.6 0.0 copy-start
  0.6 0.9 copy-done
  1.5 0.0 copy-start.1
  1.5 1.0 shard_map.41
  2.6 6.9 %all-to-all-start = ((f32[8,64,512]{2,1,0:T(8,128)}), f32[8,64,512]{2,1,0:T(8,128)S(1)}, u32[]{:S(2)}, u32[]{:S(2)}) async-start(f32[8,64,512]{2,1,0:T(8,128)} %shard_map.41), calls=%async_computation | async-start | bytes 2097152 | tf_op jit(solution)/shard_map/all_to_all | solution.py:276
  9.5 0.0 copy-done.1
  9.5 2.8 collective-permute-start.1
  12.3 0.3 collective-permute-start
  12.6 2.4 collective-permute-start.2
  15.0 9.0 %all-to-all-done.y_ref = f32[8,64,512]{2,1,0:T(8,128)S(1)} async-done(((f32[8,64,512]{2,1,0:T(8,128)}), f32[8,64,512]{2,1,0:T(8,128)S(1)}, u32[]{:S(2)}, u32[]{:S(2)}) %all-to-all-start) | async-done | bytes 1048608 | tf_op jit(solution)/shard_map/all_to_all | solution.py:276
  23.9 30.2 %shard_map.42 = (bf16[4096,128]{1,0:T(8,128)(2,1)S(1)}, bf16[4096,128]{1,0:T(8,128)(2,1)S(1)}, bf16[192,4096]{1,0:T(8,128)(2,1)S(1)}, f32[32,128]{1,0:T(8,128)S(...) custom-call(f32[64,1024]{1,0:T(8,128)S(1)} %copy-done.1, ...), custom_call_target="tpu_custom_call" | custom-call | flops 2147483648 | bytes 524288 | tf_op jit(solution)/shard_map/pallas_call | solution.py:316
  54.2 0.0 collective-permute-done.1.refs_2_
  54.2 0.0 collective-permute-done.refs_1_
  54.2 0.0 collective-permute-done.2.refs_3_
  54.2 87.6 %shard_map.43 = (bf16[4096,128]{1,0:T(8,128)(2,1)S(1)}, bf16[4096,128]{1,0:T(8,128)(2,1)S(1)}, bf16[192,4096]{1,0:T(8,128)(2,1)S(1)}, f32[32,128]{1,0:T(8,128)S(1)}, f32[16,32,128]{2,1,0:T(8,128)S(1)}) custom-call(s32[1]{0:T(128)} %bitcast.refs_0_, f32[64,1024]{1,0:T(8,128)S(1)} %collective-permute-done.refs_1_, ...), custom_call_target="tpu_custom_call" | custom-call | flops 6442450944 | bytes 1572864 | tf_op jit(solution)/shard_map/pallas_call | solution.py:328
  141.8 17.3 %all_to_all.25.parts = f32[16,32,128]{2,1,0:T(8,128)S(1)} all-to-all(f32[16,32,128]{2,1,0:T(8,128)S(1)} %get-tuple-element.33), channel_id=1, replica_groups=mesh['yh'=2,'core'=2,'x'=4,'z'=4,'yl'=2] {'yh','core','x'}, dimensions={0} | all-to-all | bytes 524288 | tf_op jit(solution)/shard_map/all_to_all | solution.py:280
  159.2 116.7 %shard_map.44 = (f32[8,32,128]{2,1,0:T(8,128)S(1)}, f32[32,128]{1,0:T(8,128)S(1)}) custom-call(f32[16,32,128]{2,1,0:T(8,128)S(1)} %all_to_all.25.parts, f32[32,128]{1,0:T(8,128)S(1)} %get-tuple-element.34.prev, bf16[4096,128]{1,0:T(8,128)(2,1)S(1)} %get-tuple-element.35.refs_0_.refs_1_, bf16[4096,128]{1,0:T(8,128)(2,1)S(1)} %get-tuple-element.36.refs_1_.refs_2_, ...), custom_call_target="tpu_custom_call" | custom-call | tf_op jit(solution)/shard_map/pallas_call | solution.py:245
  275.9 8.1 %all_to_all.26.parts = f32[8,32,128]{2,1,0:T(8,128)S(1)} all-to-all(f32[8,32,128]{2,1,0:T(8,128)S(1)} %get-tuple-element.38), channel_id=1, replica_groups=mesh['yh'=2,'core'=2,'x'=4,'z'=4,'yl'=2] {'z','yl'}, dimensions={0} | all-to-all | bytes 262144 | tf_op jit(solution)/shard_map/all_to_all | solution.py:280
  284.0 116.5 %shard_map.45 = (f32[16,32,128]{2,1,0:T(8,128)S(1)}, f32[32,128]{1,0:T(8,128)S(1)}) custom-call(f32[8,32,128]{2,1,0:T(8,128)S(1)} %all_to_all.26.parts, f32[32,128]{1,0:T(8,128)S(1)} %get-tuple-element.39.prev, bf16[4096,128]{1,0:T(8,128)(2,1)S(1)} %get-tuple-element.26.refs_4_.refs_0_, bf16[4096,128]{1,0:T(8,128)(2,1)S(1)} %get-tuple-element.40.refs_1_, ...), custom_call_target="tpu_custom_call" | custom-call | tf_op jit(solution)/shard_map/pallas_call | solution.py:245
  400.5 13.5 %all_to_all.27.parts = f32[16,32,128]{2,1,0:T(8,128)S(1)} all-to-all(f32[16,32,128]{2,1,0:T(8,128)S(1)} %get-tuple-element.42), channel_id=1, replica_groups=mesh['yh'=2,'core'=2,'x'=4,'z'=4,'yl'=2] {'yh','core','x'}, dimensions={0} | all-to-all | bytes 524288 | tf_op jit(solution)/shard_map/all_to_all | solution.py:280
  414.0 10.6 %shard_map.46 = (f32[32,32,128]{2,1,0:T(8,128)S(1)}, f32[32,128]{1,0:T(8,128)S(1)}) custom-call(f32[16,32,128]{2,1,0:T(8,128)S(1)} %all_to_all.27.parts, f32[32,128]{1,0:T(8,128)S(1)} %get-tuple-element.43.prev, f32[32,128]{1,0:T(8,128)S(1)} %get-tuple-element.44.refs_0_, bf16[4096,128]{1,0:T(8,128)(2,1)S(1)} %get-tuple-element.35.refs_0_.refs_1_, ...), custom_call_target="tpu_custom_call" | custom-call | tf_op jit(solution)/shard_map/pallas_call | solution.py:245
  424.6 14.0 %all_to_all.28.refs_1_ = f32[32,32,128]{2,1,0:T(8,128)S(1)} all-to-all(f32[32,32,128]{2,1,0:T(8,128)S(1)} %get-tuple-element.45), channel_id=1, replica_groups=mesh['yh'=2,'core'=2,'x'=4,'z'=4,'yl'=2] {'x','z','yl'}, dimensions={0} | all-to-all | bytes 1048576 | tf_op jit(solution)/shard_map/all_to_all | solution.py:280
  438.6 0.7 shard_map.47
Async XLA Ops:
  0.6 0.9 copy-start
  1.5 7.9 %copy-start.1 = (f32[64,1024]{1,0:T(8,128)S(1)}, f32[64,1024]{1,0:T(8,128)}, u32[]{:S(2)}) copy-start(f32[64,1024]{1,0:T(8,128)} %x_ref.1) | copy-start | bytes 786436
  2.6 21.4 %all-to-all-start = ((f32[8,64,512]{2,1,0:T(8,128)}), f32[8,64,512]{2,1,0:T(8,128)S(1)}, u32[]{:S(2)}, u32[]{:S(2)}) async-start(f32[8,64,512]{2,1,0:T(8,128)} %shard_map.41), calls=%async_computation | async-start | bytes 2097152 | tf_op jit(solution)/shard_map/all_to_all | solution.py:276
  9.5 44.7 %collective-permute-start.1 = (f32[64,1024]{1,0:T(8,128)S(1)}, f32[64,1024]{1,0:T(8,128)S(1)}, u32[]{:S(2)}, u32[]{:S(2)}) collective-permute-start(f32[64,1024]{1,0:T(8,128)S(1)} %copy-done.1), channel_id=1, source_target_pairs={{0,16},{8,24},{16,0},{24,8},{1,17},{9,25},{17,1},{25,9},{2,18},{10... | collective-permute-start | bytes 786440 | tf_op jit(solution)/shard_map/ppermute | solution.py:296
  12.3 41.9 %collective-permute-start = (f32[64,1024]{1,0:T(8,128)S(1)}, f32[64,1024]{1,0:T(8,128)S(1)}, u32[]{:S(2)}, u32[]{:S(2)}) collective-permute-start(f32[64,1024]{1,0:T(8,128)S(1)} %copy-done.1), channel_id=1, source_target_pairs={{0,8},{8,16},{16,24},{24,0},{1,9},{9,17},{17,25},{25,1},{2,10},{10... | collective-permute-start | bytes 786440 | tf_op jit(solution)/shard_map/ppermute | solution.py:296
  12.6 41.6 %collective-permute-start.2 = (f32[64,1024]{1,0:T(8,128)S(1)}, f32[64,1024]{1,0:T(8,128)S(1)}, u32[]{:S(2)}, u32[]{:S(2)}) collective-permute-start(f32[64,1024]{1,0:T(8,128)S(1)} %copy-done.1), channel_id=1, source_target_pairs={{0,24},{8,0},{16,8},{24,16},{1,25},{9,1},{17,9},{25,17},{2,26},{10... | collective-permute-start | bytes 786440 | tf_op jit(solution)/shard_map/ppermute | solution.py:296

commit v7 on v6

--- a/solution.py
+++ b/solution.py
@@ -16,7 +16,7 @@
 LANES = 128
 CHUNK = 256
 WIDTH = 256
-GROUP = 4
+GROUP = 8
 ACC_ROWS = 16
 DUAL_LANE = 64
 EDGE = 64
@@ -118,16 +118,18 @@
 
     zero = jnp.zeros((ACC_ROWS, WIDTH), f32)
 
+    size = min(GROUP, count)
+
     def step(group, carry):
-        for t in range(GROUP):
-            block, acc = group * GROUP + t, zero
+        for t in range(size):
+            block, acc = group * size + t, zero
             for chunk in range(chunks):
                 acc = fold(jnp.add, acc, jnp.exp2(scores(low + block, chunk)))
             here = pl.ds(pl.multiple_of(block * SUBLANES, SUBLANES), SUBLANES)
             partial[here, :] = fold(jnp.add, acc[:SUBLANES], acc[SUBLANES:])
         return carry
 
-    lax.fori_loop(0, count // GROUP, step, 0)
+    lax.fori_loop(0, count // size, step, 0)
     least = jnp.full((1, WIDTH), 1.0, f32)
     for block in range(count):
         total = jnp.sum(partial[block * SUBLANES : (block + 1) * SUBLANES, :], axis=0, keepdims=True)
@@ -260,17 +262,22 @@
     )(parts, prev, *norms, main, tail, rhs)
 
 
-def repeat_kernel(value, out):
-    for i in range(out.shape[0]):
-        out[i] = value[...]
+def repeat_kernel(value, out, done):
+    copies = [pltpu.make_async_copy(value, out.at[i], done.at[i]) for i in range(out.shape[0])]
+    for copy in copies:
+        copy.start()
+    for copy in copies:
+        copy.wait()
 
 
 def gathered(value, axes):
+    count = lax.axis_size(axes)
     copies = pl.pallas_call(
         repeat_kernel,
-        out_shape=jax.ShapeDtypeStruct((lax.axis_size(axes),) + value.shape, value.dtype),
-        in_specs=[vmem],
-        out_specs=vmem,
+        out_shape=jax.ShapeDtypeStruct((count,) + value.shape, value.dtype),
+        in_specs=[pl.BlockSpec(memory_space=pl.ANY)],
+        out_specs=pl.BlockSpec(memory_space=pl.ANY),
+        scratch_shapes=[pltpu.SemaphoreType.DMA((count,))],
         compiler_params=params(4),
     )(value)
     return lax.all_to_all(copies, axes, 0, 0, tiled=True)

time: 440 us -> 542 us (1.23)
  the two profiles are of different devices: /device:TPU:1 before, /device:TPU:16 now
where the time goes in v7:
time: 542 us
  Pallas kernels  362 us (67%)
  blocking collectives  156 us (29%)
  starting transfers between devices  12.4 us (2%)
  waiting for transfers between devices  9.36 us (2%)
    pallas_call x3, Pallas kernels, lse_pass(): pl.pallas_call(kernel, out_shape=(jax.ShapeDtypeStruct((copies, width //...  242 us
    all_to_all x4, blocking collectives, exchanged(): return lax.all_to_all(parts, axes, 0, 0, tiled=True)  156 us
    pallas_call x1, Pallas kernels, on_device(): pl.pallas_call(lambda *refs: second_kernel(ring, *refs), out_shape=side(r...  87.6 us
    pallas_call x1, Pallas kernels, on_device(): pl.pallas_call(first_kernel, out_shape=side(cols) + [jax.ShapeDtypeStruct...  30.2 us
  transfers between devices with their start and end apart: 4, of which 1 were waited for; matrix products, arithmetic and copies ran while one was open for 0% of the time, Pallas kernels for 6%

profile of v7, /device:TPU:16, one launch (start us, length us, event | category | flops | bytes accessed | tf_op | source)
XLA Modules:
  0.0 541.8 jit_solution(16959854745723334754)
XLA Ops:
  0.6 0.0 copy-start
  0.6 0.9 copy-done
  1.5 0.0 copy-start.1
  1.5 1.0 shard_map.41
  2.6 6.0 %all-to-all-start = ((f32[8,64,512]{2,1,0:T(8,128)}), f32[8,64,512]{2,1,0:T(8,128)S(1)}, u32[]{:S(2)}, u32[]{:S(2)}) async-start(f32[8,64,512]{2,1,0:T(8,128)} %shard_map.41), calls=%async_computation | async-start | bytes 2097152 | tf_op jit(solution)/shard_map/all_to_all | solution.py:283
  8.6 0.0 copy-done.1
  8.6 3.1 collective-permute-start.1
  11.7 0.6 collective-permute-start
  12.3 2.6 collective-permute-start.2
  15.0 9.4 %all-to-all-done.y_ref = f32[8,64,512]{2,1,0:T(8,128)S(1)} async-done(((f32[8,64,512]{2,1,0:T(8,128)}), f32[8,64,512]{2,1,0:T(8,128)S(1)}, u32[]{:S(2)}, u32[]{:S(2)}) %all-to-all-start) | async-done | bytes 1048608 | tf_op jit(solution)/shard_map/all_to_all | solution.py:283
  24.3 30.2 %shard_map.42 = (bf16[4096,128]{1,0:T(8,128)(2,1)S(1)}, bf16[4096,128]{1,0:T(8,128)(2,1)S(1)}, bf16[192,4096]{1,0:T(8,128)(2,1)S(1)}, f32[32,128]{1,0:T(8,128)S(...) custom-call(f32[64,1024]{1,0:T(8,128)S(1)} %copy-done.1, ...), custom_call_target="tpu_custom_call" | custom-call | flops 2147483648 | bytes 524288 | tf_op jit(solution)/shard_map/pallas_call | solution.py:323
  54.6 0.0 collective-permute-done.1.refs_2_
  54.6 0.0 collective-permute-done.refs_1_
  54.6 0.0 collective-permute-done.2.refs_3_
  54.6 87.6 %shard_map.43 = (bf16[4096,128]{1,0:T(8,128)(2,1)S(1)}, bf16[4096,128]{1,0:T(8,128)(2,1)S(1)}, bf16[192,4096]{1,0:T(8,128)(2,1)S(1)}, f32[32,128]{1,0:T(8,128)S(1)}, f32[16,32,128]{2,1,0:T(8,128)S(1)}) custom-call(s32[1]{0:T(128)} %bitcast.refs_0_, f32[64,1024]{1,0:T(8,128)S(1)} %collective-permute-done.refs_1_, ...), custom_call_target="tpu_custom_call" | custom-call | flops 6442450944 | bytes 1572864 | tf_op jit(solution)/shard_map/pallas_call | solution.py:335
  142.2 13.6 %all_to_all.25.parts = f32[16,32,128]{2,1,0:T(8,128)S(1)} all-to-all(f32[16,32,128]{2,1,0:T(8,128)S(1)} %get-tuple-element.33), channel_id=1, replica_groups=mesh['yh'=2,'core'=2,'x'=4,'z'=4,'yl'=2] {'yh','core','x'}, dimensions={0} | all-to-all | bytes 524288 | tf_op jit(solution)/shard_map/all_to_all | solution.py:287
  155.8 116.2 %shard_map.44 = (f32[8,32,128]{2,1,0:T(8,128)S(1)}, f32[32,128]{1,0:T(8,128)S(1)}) custom-call(f32[16,32,128]{2,1,0:T(8,128)S(1)} %all_to_all.25.parts, f32[32,128]{1,0:T(8,128)S(1)} %get-tuple-element.34.prev, bf16[4096,128]{1,0:T(8,128)(2,1)S(1)} %get-tuple-element.35.refs_0_.refs_1_, bf16[4096,128]{1,0:T(8,128)(2,1)S(1)} %get-tuple-element.36.refs_1_.refs_2_, ...), custom_call_target="tpu_custom_call" | custom-call | tf_op jit(solution)/shard_map/pallas_call | solution.py:247
  272.0 9.2 %all_to_all.26.parts = f32[8,32,128]{2,1,0:T(8,128)S(1)} all-to-all(f32[8,32,128]{2,1,0:T(8,128)S(1)} %get-tuple-element.38), channel_id=1, replica_groups=mesh['yh'=2,'core'=2,'x'=4,'z'=4,'yl'=2] {'z','yl'}, dimensions={0} | all-to-all | bytes 262144 | tf_op jit(solution)/shard_map/all_to_all | solution.py:287
  281.3 116.1 %shard_map.45 = (f32[16,32,128]{2,1,0:T(8,128)S(1)}, f32[32,128]{1,0:T(8,128)S(1)}) custom-call(f32[8,32,128]{2,1,0:T(8,128)S(1)} %all_to_all.26.parts, f32[32,128]{1,0:T(8,128)S(1)} %get-tuple-element.39.prev, bf16[4096,128]{1,0:T(8,128)(2,1)S(1)} %get-tuple-element.26.refs_4_.refs_0_, bf16[4096,128]{1,0:T(8,128)(2,1)S(1)} %get-tuple-element.40.refs_1_, ...), custom_call_target="tpu_custom_call" | custom-call | tf_op jit(solution)/shard_map/pallas_call | solution.py:247
  397.4 12.2 %all_to_all.27.parts = f32[16,32,128]{2,1,0:T(8,128)S(1)} all-to-all(f32[16,32,128]{2,1,0:T(8,128)S(1)} %get-tuple-element.42), channel_id=1, replica_groups=mesh['yh'=2,'core'=2,'x'=4,'z'=4,'yl'=2] {'yh','core','x'}, dimensions={0} | all-to-all | bytes 524288 | tf_op jit(solution)/shard_map/all_to_all | solution.py:287
  409.6 10.1 %shard_map.46 = (f32[32,32,128]{2,1,0:T(8,128)S(1)}, f32[32,128]{1,0:T(8,128)S(1)}) custom-call(f32[16,32,128]{2,1,0:T(8,128)S(1)} %all_to_all.27.parts, f32[32,128]{1,0:T(8,128)S(1)} %get-tuple-element.43.prev, f32[32,128]{1,0:T(8,128)S(1)} %get-tuple-element.44.refs_0_, bf16[4096,128]{1,0:T(8,128)(2,1)S(1)} %get-tuple-element.35.refs_0_.refs_1_, ...), custom_call_target="tpu_custom_call" | custom-call | tf_op jit(solution)/shard_map/pallas_call | solution.py:247
  419.7 121.4 %all_to_all.28.refs_1_ = f32[32,32,128]{2,1,0:T(8,128)S(1)} all-to-all(f32[32,32,128]{2,1,0:T(8,128)S(1)} %get-tuple-element.45), channel_id=1, replica_groups=mesh['yh'=2,'core'=2,'x'=4,'z'=4,'yl'=2] {'x','z','yl'}, dimensions={0} | all-to-all | bytes 1048576 | tf_op jit(solution)/shard_map/all_to_all | solution.py:287
  541.1 0.7 shard_map.47
Async XLA Ops:
  0.6 0.9 copy-start
  1.5 7.1 %copy-start.1 = (f32[64,1024]{1,0:T(8,128)S(1)}, f32[64,1024]{1,0:T(8,128)}, u32[]{:S(2)}) copy-start(f32[64,1024]{1,0:T(8,128)} %x_ref.1) | copy-start | bytes 786436
  2.6 21.7 %all-to-all-start = ((f32[8,64,512]{2,1,0:T(8,128)}), f32[8,64,512]{2,1,0:T(8,128)S(1)}, u32[]{:S(2)}, u32[]{:S(2)}) async-start(f32[8,64,512]{2,1,0:T(8,128)} %shard_map.41), calls=%async_computation | async-start | bytes 2097152 | tf_op jit(solution)/shard_map/all_to_all | solution.py:283
  8.6 45.9 %collective-permute-start.1 = (f32[64,1024]{1,0:T(8,128)S(1)}, f32[64,1024]{1,0:T(8,128)S(1)}, u32[]{:S(2)}, u32[]{:S(2)}) collective-permute-start(f32[64,1024]{1,0:T(8,128)S(1)} %copy-done.1), channel_id=1, source_target_pairs={{0,16},{8,24},{16,0},{24,8},{1,17},{9,25},{17,1},{25,9},{2,18},{10... | collective-permute-start | bytes 786440 | tf_op jit(solution)/shard_map/ppermute | solution.py:303
  11.7 42.8 %collective-permute-start = (f32[64,1024]{1,0:T(8,128)S(1)}, f32[64,1024]{1,0:T(8,128)S(1)}, u32[]{:S(2)}, u32[]{:S(2)}) collective-permute-start(f32[64,1024]{1,0:T(8,128)S(1)} %copy-done.1), channel_id=1, source_target_pairs={{0,8},{8,16},{16,24},{24,0},{1,9},{9,17},{17,25},{25,1},{2,10},{10... | collective-permute-start | bytes 786440 | tf_op jit(solution)/shard_map/ppermute | solution.py:303
  12.3 42.2 %collective-permute-start.2 = (f32[64,1024]{1,0:T(8,128)S(1)}, f32[64,1024]{1,0:T(8,128)S(1)}, u32[]{:S(2)}, u32[]{:S(2)}) collective-permute-start(f32[64,1024]{1,0:T(8,128)S(1)} %copy-done.1), channel_id=1, source_target_pairs={{0,24},{8,0},{16,8},{24,16},{1,25},{9,1},{17,9},{25,17},{2,26},{10... | collective-permute-start | bytes 786440 | tf_op jit(solution)/shard_map/ppermute | solution.py:303
